TPU v7x, 256 devices: a whole 4x4x8 slice. The times are simulated.
256 devices in a mesh: blk: 64 (over z, x_hi, y), group: 4 (over x_lo, core).
Axes of the slice: x: 4 (x_hi: 2, x_lo: 2; x = x_hi * 2 + x_lo), y: 4, z: 8, core: 2. Of those that a mesh axis runs over, the one named last changes fastest.
Arguments:
- image_embeds: bfloat16 [4, 6144, 1152], P('group', 'blk')
- text_embeds: bfloat16 [4, 6144, 1152], P('group', 'blk'), may hold values from -0.1875 to 0.1875
- positives: int32 [4, 6144], P('group', 'blk'), may hold values from 0 to 6143, each once within a row
- partner: int32 [4], replicated, may hold values from 0 to 3, each once
- log_temp: float32 [1], replicated, may hold values from 1.6 to 2.4
- bias: float32 [1], replicated, may hold values from -4 to -2
Outputs:
- image_grads: float32 [4, 6144, 1152], P('group', 'blk')
- text_grads: float32 [4, 6144, 1152], P('group', 'blk')
- loss: float32 [1], replicated
Inputs may be any that keep to these rules, and one draw needn't show every extreme that they name: Each group's positives name every text row of its partner group exactly once. `partner`: every group is named exactly once.
All inputs are finite; a program needn't handle non-finite values.
Results may differ from a plain program's by a relative error of at most 0.0015.
Values may be sent and summed in bfloat16 or wider, within the bound.
A program may use at most 64 MiB of HBM per device.

v0:
```python
import jax
import jax.numpy as jnp
from jax import lax
from jax.sharding import PartitionSpec as P


def shifted(array, axis, by):
    size = lax.axis_size(axis)
    return lax.ppermute(array, axis, [(i, (i + by) % size) for i in range(size)])


def pair_block(images, texts, hits, temper, offset):
    logits = temper * jnp.dot(images, texts.T, preferred_element_type=jnp.float32) + offset
    hit_values = hits.astype(jnp.float32)
    losses = jax.nn.softplus(logits) - hit_values * logits
    slopes = (jax.nn.sigmoid(logits) - hit_values).astype(jnp.bfloat16)
    return (jnp.sum(losses), slopes)


def shards(image_embeds, text_embeds, positives, partner, log_temp, bias):
    temper = jnp.exp(log_temp[0])
    offset = bias[0]
    images = image_embeds[0]
    own_texts = text_embeds[0]
    own_labels = positives[0]
    rows = images.shape[0]
    width = images.shape[1]
    cycle_size = lax.axis_size("blk")
    group_count = lax.axis_size("group")
    blk_place = lax.axis_index("blk")
    group_place = lax.axis_index("group")
    every_text = lax.all_gather(own_texts, "group", axis=0, tiled=True)
    target = partner[group_place]
    partner_block = lax.dynamic_slice_in_dim(every_text, target * rows, rows, 0)
    columns = jnp.arange(rows, dtype=jnp.int32)

    def hits_for(labels, source):
        return labels[:, None] == (source * rows + columns)[None, :]

    def work(visit_images, visit_texts, visit_labels, source, image_sum, text_sum, total):
        part, slopes = pair_block(images, visit_texts, hits_for(own_labels, source), temper, offset)
        image_sum = image_sum + temper * jnp.dot(
            slopes, visit_texts, preferred_element_type=jnp.float32
        )
        unused, back_slopes = pair_block(
            visit_images, partner_block, hits_for(visit_labels, blk_place), temper, offset
        )
        text_sum = text_sum + temper * jnp.dot(
            back_slopes.T, visit_images, preferred_element_type=jnp.float32
        )
        return (image_sum, text_sum, total + part)

    zero_block = jnp.zeros((rows, width), jnp.float32)
    zero_total = jnp.zeros((), jnp.float32)

    def advance(step, carry):
        visit_images, visit_texts, visit_labels, image_sum, text_sum, total = carry
        source = (blk_place - step) % cycle_size
        image_sum, text_sum, total = work(
            visit_images, visit_texts, visit_labels, source, image_sum, text_sum, total
        )
        visit_images, visit_texts = shifted((visit_images, visit_texts), "blk", 1)
        visit_labels = shifted(visit_labels, "blk", 1)
        return (visit_images, visit_texts, visit_labels, image_sum, text_sum, total)

    start = (images, partner_block, own_labels, zero_block, zero_block, zero_total)
    finished = lax.fori_loop(0, cycle_size, advance, start)
    image_sum = finished[3]
    text_sum = finished[4]
    total = finished[5]
    spread = jnp.zeros((group_count * rows, width), jnp.float32)
    spread = lax.dynamic_update_slice_in_dim(spread, text_sum, target * rows, 0)
    text_home = lax.psum_scatter(spread, "group", scatter_dimension=0, tiled=True)
    total = lax.psum(total, ("blk", "group"))
    loss = total / (group_count * rows * cycle_size * cycle_size)
    return (image_sum[None], text_home[None], jnp.reshape(loss, (1,)))


def solution(mesh):
    in_specs = (P("group", "blk", None), P("group", "blk", None), P("group", "blk"), P(), P(), P())
    out_specs = (P("group", "blk", None), P("group", "blk", None), P())
    return jax.shard_map(shards, mesh=mesh, in_specs=in_specs, out_specs=out_specs, check_vma=False)
```

profile of v0, /device:TPU:1, one launch (start us, length us, event | category | flops | bytes accessed | tf_op | source)
XLA Modules:
  0.0 1113.0 jit_solution(16523229869733147264)
XLA Ops:
  11.5 10.8 all-gather
  22.3 943.6 %while.27 = (s32[]{:T(128)}, bf16[96,1152]{1,0:T(8,128)(2,1)S(1)}, bf16[96,1152]{1,0:T(8,128)(2,1)S(1)}, s32[96]{0:T(128)S(1)}, f32[96,1152]{1,0:T(8,128)S(1)}, ...) while((s32[]{:T(128)}, bf16[96,1152]{1,0:T(8,128)(2,1)S(1)}, ...), condition=%wide.region_2.3_spmd.clone.clone, body=%wide.region_0.2_spmd.clone.clone.sunk | while | flops 85856464 | bytes 5609185 | solution.py:67
  33.4 4.8 collective-permute-done
  38.3 4.7 collective-permute-done.1
  71.0 4.7 collective-permute-done.1
  207.6 4.9 collective-permute-done
  223.8 4.9 collective-permute-done
  245.3 4.7 collective-permute-done.1
  276.9 4.8 collective-permute-done.1
  398.2 4.9 collective-permute-done
  413.9 4.9 collective-permute-done
  430.4 4.9 collective-permute-done
  435.3 4.7 collective-permute-done.1
  452.2 4.7 collective-permute-done.1
  604.8 4.9 collective-permute-done
  620.8 4.8 collective-permute-done
  658.8 4.7 collective-permute-done.1
  674.4 4.8 collective-permute-done.1
  795.7 4.9 collective-permute-done
  811.1 4.9 collective-permute-done
  827.3 5.2 collective-permute-done
  865.9 4.7 collective-permute-done.1
  881.2 4.7 collective-permute-done.1
  967.3 137.1 %psum.7 = f32[]{:T(128)} all-reduce(f32[]{:T(128)} %get-tuple-element.347), channel_id=1, replica_groups=mesh['blk'=64,'group'=4] {'blk','group'}, use_global_device_ids=true, to_apply=%region_4.5 | all-reduce | flops 1 | bytes 8 | tf_op jit(solution)/shard_map/psum | solution.py:74
  (895 shorter events, 801.4 us)
Async XLA Ops:
  7.2 1097.9 %reduce-scatter.2.cloned.1.call-start = ((), (), s32[]{:S(2)}) async-start(), calls=%async_computation.1 | async-start | bytes 2211840 | tf_op jit(solution)/shard_map/reduce_scatter | solution.py:73
  25.0 18.0 %collective-permute-start.1 = (bf16[96,1152]{1,0:T(8,128)(2,1)S(1)}, bf16[96,1152]{1,0:T(8,128)(2,1)S(1)}, u32[]{:S(2)}, u32[]{:S(2)}) collective-permute-start(bf16[96,1152]{1,0:T(8,128)(2,1)S(1)} %copy.18), channel_id=1, source_target_pairs={{0,4},{4,8},{8,12},{12,16},{16,20},{20,24},{24,28},{28,32},{32,36}... | collective-permute-start | bytes 663560 | tf_op jit(solution)/shard_map/while/body/eval_jaxpr/ppermute | solution.py:9
  43.2 16.7 %collective-permute-start.1 = (bf16[96,1152]{1,0:T(8,128)(2,1)S(1)}, bf16[96,1152]{1,0:T(8,128)(2,1)S(1)}, u32[]{:S(2)}, u32[]{:S(2)}) collective-permute-start(bf16[96,1152]{1,0:T(8,128)(2,1)S(1)} %copy.18), channel_id=1, source_target_pairs={{0,4},{4,8},{8,12},{12,16},{16,20},{20,24},{24,28},{28,32},{32,36}... | collective-permute-start | bytes 663560 | tf_op jit(solution)/shard_map/while/body/eval_jaxpr/ppermute | solution.py:9
  60.0 15.8 %collective-permute-start.1 = (bf16[96,1152]{1,0:T(8,128)(2,1)S(1)}, bf16[96,1152]{1,0:T(8,128)(2,1)S(1)}, u32[]{:S(2)}, u32[]{:S(2)}) collective-permute-start(bf16[96,1152]{1,0:T(8,128)(2,1)S(1)} %copy.18), channel_id=1, source_target_pairs={{0,4},{4,8},{8,12},{12,16},{16,20},{20,24},{24,28},{28,32},{32,36}... | collective-permute-start | bytes 663560 | tf_op jit(solution)/shard_map/while/body/eval_jaxpr/ppermute | solution.py:9
  199.2 16.2 %collective-permute-start.1 = (bf16[96,1152]{1,0:T(8,128)(2,1)S(1)}, bf16[96,1152]{1,0:T(8,128)(2,1)S(1)}, u32[]{:S(2)}, u32[]{:S(2)}) collective-permute-start(bf16[96,1152]{1,0:T(8,128)(2,1)S(1)} %copy.18), channel_id=1, source_target_pairs={{0,4},{4,8},{8,12},{12,16},{16,20},{20,24},{24,28},{28,32},{32,36}... | collective-permute-start | bytes 663560 | tf_op jit(solution)/shard_map/while/body/eval_jaxpr/ppermute | solution.py:9
  215.6 17.3 %collective-permute-start.1 = (bf16[96,1152]{1,0:T(8,128)(2,1)S(1)}, bf16[96,1152]{1,0:T(8,128)(2,1)S(1)}, u32[]{:S(2)}, u32[]{:S(2)}) collective-permute-start(bf16[96,1152]{1,0:T(8,128)(2,1)S(1)} %copy.18), channel_id=1, source_target_pairs={{0,4},{4,8},{8,12},{12,16},{16,20},{20,24},{24,28},{28,32},{32,36}... | collective-permute-start | bytes 663560 | tf_op jit(solution)/shard_map/while/body/eval_jaxpr/ppermute | solution.py:9
  233.0 17.1 %collective-permute-start.1 = (bf16[96,1152]{1,0:T(8,128)(2,1)S(1)}, bf16[96,1152]{1,0:T(8,128)(2,1)S(1)}, u32[]{:S(2)}, u32[]{:S(2)}) collective-permute-start(bf16[96,1152]{1,0:T(8,128)(2,1)S(1)} %copy.18), channel_id=1, source_target_pairs={{0,4},{4,8},{8,12},{12,16},{16,20},{20,24},{24,28},{28,32},{32,36}... | collective-permute-start | bytes 663560 | tf_op jit(solution)/shard_map/while/body/eval_jaxpr/ppermute | solution.py:9
  250.2 16.1 %collective-permute-start.1 = (bf16[96,1152]{1,0:T(8,128)(2,1)S(1)}, bf16[96,1152]{1,0:T(8,128)(2,1)S(1)}, u32[]{:S(2)}, u32[]{:S(2)}) collective-permute-start(bf16[96,1152]{1,0:T(8,128)(2,1)S(1)} %copy.18), channel_id=1, source_target_pairs={{0,4},{4,8},{8,12},{12,16},{16,20},{20,24},{24,28},{28,32},{32,36}... | collective-permute-start | bytes 663560 | tf_op jit(solution)/shard_map/while/body/eval_jaxpr/ppermute | solution.py:9
  266.4 15.2 %collective-permute-start.1 = (bf16[96,1152]{1,0:T(8,128)(2,1)S(1)}, bf16[96,1152]{1,0:T(8,128)(2,1)S(1)}, u32[]{:S(2)}, u32[]{:S(2)}) collective-permute-start(bf16[96,1152]{1,0:T(8,128)(2,1)S(1)} %copy.18), channel_id=1, source_target_pairs={{0,4},{4,8},{8,12},{12,16},{16,20},{20,24},{24,28},{28,32},{32,36}... | collective-permute-start | bytes 663560 | tf_op jit(solution)/shard_map/while/body/eval_jaxpr/ppermute | solution.py:9
  389.9 15.6 %collective-permute-start.1 = (bf16[96,1152]{1,0:T(8,128)(2,1)S(1)}, bf16[96,1152]{1,0:T(8,128)(2,1)S(1)}, u32[]{:S(2)}, u32[]{:S(2)}) collective-permute-start(bf16[96,1152]{1,0:T(8,128)(2,1)S(1)} %copy.18), channel_id=1, source_target_pairs={{0,4},{4,8},{8,12},{12,16},{16,20},{20,24},{24,28},{28,32},{32,36}... | collective-permute-start | bytes 663560 | tf_op jit(solution)/shard_map/while/body/eval_jaxpr/ppermute | solution.py:9
  405.6 16.6 %collective-permute-start.1 = (bf16[96,1152]{1,0:T(8,128)(2,1)S(1)}, bf16[96,1152]{1,0:T(8,128)(2,1)S(1)}, u32[]{:S(2)}, u32[]{:S(2)}) collective-permute-start(bf16[96,1152]{1,0:T(8,128)(2,1)S(1)} %copy.18), channel_id=1, source_target_pairs={{0,4},{4,8},{8,12},{12,16},{16,20},{20,24},{24,28},{28,32},{32,36}... | collective-permute-start | bytes 663560 | tf_op jit(solution)/shard_map/while/body/eval_jaxpr/ppermute | solution.py:9
  422.4 17.7 %collective-permute-start.1 = (bf16[96,1152]{1,0:T(8,128)(2,1)S(1)}, bf16[96,1152]{1,0:T(8,128)(2,1)S(1)}, u32[]{:S(2)}, u32[]{:S(2)}) collective-permute-start(bf16[96,1152]{1,0:T(8,128)(2,1)S(1)} %copy.18), channel_id=1, source_target_pairs={{0,4},{4,8},{8,12},{12,16},{16,20},{20,24},{24,28},{28,32},{32,36}... | collective-permute-start | bytes 663560 | tf_op jit(solution)/shard_map/while/body/eval_jaxpr/ppermute | solution.py:9
  440.2 16.8 %collective-permute-start.1 = (bf16[96,1152]{1,0:T(8,128)(2,1)S(1)}, bf16[96,1152]{1,0:T(8,128)(2,1)S(1)}, u32[]{:S(2)}, u32[]{:S(2)}) collective-permute-start(bf16[96,1152]{1,0:T(8,128)(2,1)S(1)} %copy.18), channel_id=1, source_target_pairs={{0,4},{4,8},{8,12},{12,16},{16,20},{20,24},{24,28},{28,32},{32,36}... | collective-permute-start | bytes 663560 | tf_op jit(solution)/shard_map/while/body/eval_jaxpr/ppermute | solution.py:9
  457.1 15.9 %collective-permute-start.1 = (bf16[96,1152]{1,0:T(8,128)(2,1)S(1)}, bf16[96,1152]{1,0:T(8,128)(2,1)S(1)}, u32[]{:S(2)}, u32[]{:S(2)}) collective-permute-start(bf16[96,1152]{1,0:T(8,128)(2,1)S(1)} %copy.18), channel_id=1, source_target_pairs={{0,4},{4,8},{8,12},{12,16},{16,20},{20,24},{24,28},{28,32},{32,36}... | collective-permute-start | bytes 663560 | tf_op jit(solution)/shard_map/while/body/eval_jaxpr/ppermute | solution.py:9
  596.4 15.9 %collective-permute-start.1 = (bf16[96,1152]{1,0:T(8,128)(2,1)S(1)}, bf16[96,1152]{1,0:T(8,128)(2,1)S(1)}, u32[]{:S(2)}, u32[]{:S(2)}) collective-permute-start(bf16[96,1152]{1,0:T(8,128)(2,1)S(1)} %copy.18), channel_id=1, source_target_pairs={{0,4},{4,8},{8,12},{12,16},{16,20},{20,24},{24,28},{28,32},{32,36}... | collective-permute-start | bytes 663560 | tf_op jit(solution)/shard_map/while/body/eval_jaxpr/ppermute | solution.py:9
  612.5 17.0 %collective-permute-start.1 = (bf16[96,1152]{1,0:T(8,128)(2,1)S(1)}, bf16[96,1152]{1,0:T(8,128)(2,1)S(1)}, u32[]{:S(2)}, u32[]{:S(2)}) collective-permute-start(bf16[96,1152]{1,0:T(8,128)(2,1)S(1)} %copy.18), channel_id=1, source_target_pairs={{0,4},{4,8},{8,12},{12,16},{16,20},{20,24},{24,28},{28,32},{32,36}... | collective-permute-start | bytes 663560 | tf_op jit(solution)/shard_map/while/body/eval_jaxpr/ppermute | solution.py:9
  629.7 17.3 %collective-permute-start.1 = (bf16[96,1152]{1,0:T(8,128)(2,1)S(1)}, bf16[96,1152]{1,0:T(8,128)(2,1)S(1)}, u32[]{:S(2)}, u32[]{:S(2)}) collective-permute-start(bf16[96,1152]{1,0:T(8,128)(2,1)S(1)} %copy.18), channel_id=1, source_target_pairs={{0,4},{4,8},{8,12},{12,16},{16,20},{20,24},{24,28},{28,32},{32,36}... | collective-permute-start | bytes 663560 | tf_op jit(solution)/shard_map/while/body/eval_jaxpr/ppermute | solution.py:9
  647.1 16.4 %collective-permute-start.1 = (bf16[96,1152]{1,0:T(8,128)(2,1)S(1)}, bf16[96,1152]{1,0:T(8,128)(2,1)S(1)}, u32[]{:S(2)}, u32[]{:S(2)}) collective-permute-start(bf16[96,1152]{1,0:T(8,128)(2,1)S(1)} %copy.18), channel_id=1, source_target_pairs={{0,4},{4,8},{8,12},{12,16},{16,20},{20,24},{24,28},{28,32},{32,36}... | collective-permute-start | bytes 663560 | tf_op jit(solution)/shard_map/while/body/eval_jaxpr/ppermute | solution.py:9
  663.7 15.5 %collective-permute-start.1 = (bf16[96,1152]{1,0:T(8,128)(2,1)S(1)}, bf16[96,1152]{1,0:T(8,128)(2,1)S(1)}, u32[]{:S(2)}, u32[]{:S(2)}) collective-permute-start(bf16[96,1152]{1,0:T(8,128)(2,1)S(1)} %copy.18), channel_id=1, source_target_pairs={{0,4},{4,8},{8,12},{12,16},{16,20},{20,24},{24,28},{28,32},{32,36}... | collective-permute-start | bytes 663560 | tf_op jit(solution)/shard_map/while/body/eval_jaxpr/ppermute | solution.py:9
  787.4 15.3 %collective-permute-start.1 = (bf16[96,1152]{1,0:T(8,128)(2,1)S(1)}, bf16[96,1152]{1,0:T(8,128)(2,1)S(1)}, u32[]{:S(2)}, u32[]{:S(2)}) collective-permute-start(bf16[96,1152]{1,0:T(8,128)(2,1)S(1)} %copy.18), channel_id=1, source_target_pairs={{0,4},{4,8},{8,12},{12,16},{16,20},{20,24},{24,28},{28,32},{32,36}... | collective-permute-start | bytes 663560 | tf_op jit(solution)/shard_map/while/body/eval_jaxpr/ppermute | solution.py:9
  802.8 16.4 %collective-permute-start.1 = (bf16[96,1152]{1,0:T(8,128)(2,1)S(1)}, bf16[96,1152]{1,0:T(8,128)(2,1)S(1)}, u32[]{:S(2)}, u32[]{:S(2)}) collective-permute-start(bf16[96,1152]{1,0:T(8,128)(2,1)S(1)} %copy.18), channel_id=1, source_target_pairs={{0,4},{4,8},{8,12},{12,16},{16,20},{20,24},{24,28},{28,32},{32,36}... | collective-permute-start | bytes 663560 | tf_op jit(solution)/shard_map/while/body/eval_jaxpr/ppermute | solution.py:9
  819.4 17.8 %collective-permute-start.1 = (bf16[96,1152]{1,0:T(8,128)(2,1)S(1)}, bf16[96,1152]{1,0:T(8,128)(2,1)S(1)}, u32[]{:S(2)}, u32[]{:S(2)}) collective-permute-start(bf16[96,1152]{1,0:T(8,128)(2,1)S(1)} %copy.18), channel_id=1, source_target_pairs={{0,4},{4,8},{8,12},{12,16},{16,20},{20,24},{24,28},{28,32},{32,36}... | collective-permute-start | bytes 663560 | tf_op jit(solution)/shard_map/while/body/eval_jaxpr/ppermute | solution.py:9
  837.3 17.0 %collective-permute-start.1 = (bf16[96,1152]{1,0:T(8,128)(2,1)S(1)}, bf16[96,1152]{1,0:T(8,128)(2,1)S(1)}, u32[]{:S(2)}, u32[]{:S(2)}) collective-permute-start(bf16[96,1152]{1,0:T(8,128)(2,1)S(1)} %copy.18), channel_id=1, source_target_pairs={{0,4},{4,8},{8,12},{12,16},{16,20},{20,24},{24,28},{28,32},{32,36}... | collective-permute-start | bytes 663560 | tf_op jit(solution)/shard_map/while/body/eval_jaxpr/ppermute | solution.py:9
  854.5 16.1 %collective-permute-start.1 = (bf16[96,1152]{1,0:T(8,128)(2,1)S(1)}, bf16[96,1152]{1,0:T(8,128)(2,1)S(1)}, u32[]{:S(2)}, u32[]{:S(2)}) collective-permute-start(bf16[96,1152]{1,0:T(8,128)(2,1)S(1)} %copy.18), channel_id=1, source_target_pairs={{0,4},{4,8},{8,12},{12,16},{16,20},{20,24},{24,28},{28,32},{32,36}... | collective-permute-start | bytes 663560 | tf_op jit(solution)/shard_map/while/body/eval_jaxpr/ppermute | solution.py:9
  (173 other events, 1845.2 us)
Sparse Core Ops, SparseCore 0:
  967.4 88.8 reduce-scatter.1
where the time goes:
time: 1120 us; the launch traced here: 1110 us
  waiting for transfers between devices  686 us (61%)
  matrix products  195 us (17%)
  blocking collectives  148 us (13%)
  loops' own time  45.2 us (4%)
  between operations  17.3 us (2%)
  starting transfers between devices  14.4 us (1%)
    ppermute x192, waiting for transfers between devices, shifted(): lax.ppermute(array, axis, [(i, (i + by) % size) for i in range(size)])  685 us
    psum x1, blocking collectives, shards(): total = lax.psum(total, ('blk', 'group'))  137 us
    dot_general x64, matrix products, pair_block(): jnp.dot(images, texts.T, preferred_element_type=jnp.float32)  96.4 us
    dot_general x64, matrix products, work(): jnp.dot(back_slopes.T, visit_images, preferred_element_type=jnp.float32)  80.1 us
    another operation x1, loops' own time, shards(): finished = lax.fori_loop(0, cycle_size, advance, start)  45.2 us
  transfers between devices with their start and end apart: 193, of which 192 were waited for; matrix products, arithmetic and copies ran while one was open for 18% of the time, Pallas kernels for 0%

commit v1 on v0

v1 whole, which is shorter than its diff:
```python
import jax
import jax.numpy as jnp
from jax import lax
from jax.sharding import PartitionSpec as P

LINE = 8


def pair_block(images, texts, hits, temper, offset):
    logits = temper * jnp.dot(images, texts.T, preferred_element_type=jnp.float32) + offset
    hit_values = hits.astype(jnp.float32)
    losses = jax.nn.softplus(logits) - hit_values * logits
    slopes = (jax.nn.sigmoid(logits) - hit_values).astype(jnp.bfloat16)
    return (jnp.sum(losses), slopes)


def shards(image_embeds, text_embeds, positives, partner, log_temp, bias):
    temper = jnp.exp(log_temp[0])
    offset = bias[0]
    images = image_embeds[0]
    own_texts = text_embeds[0]
    own_labels = positives[0]
    rows = images.shape[0]
    width = images.shape[1]
    cycle_size = lax.axis_size("blk")
    group_count = lax.axis_size("group")
    blk_place = lax.axis_index("blk")
    group_place = lax.axis_index("group")
    down = cycle_size // LINE
    across_groups = [[a * LINE + b for b in range(LINE)] for a in range(down)]
    down_groups = [[a * LINE + b for a in range(down)] for b in range(LINE)]

    every_text = lax.all_gather(own_texts, "group", axis=0, tiled=True)
    target = partner[group_place]
    partner_block = lax.dynamic_slice_in_dim(every_text, target * rows, rows, 0)

    tile_images = lax.all_gather(images, "blk", axis=0, tiled=True, axis_index_groups=across_groups)
    tile_labels = lax.all_gather(own_labels, "blk", axis=0, tiled=True, axis_index_groups=across_groups)
    tile_texts = lax.all_gather(partner_block, "blk", axis=0, tiled=True, axis_index_groups=down_groups)
    column = jnp.arange(down * rows, dtype=jnp.int32)
    owner = (column // rows) * LINE + blk_place % LINE
    column = owner * rows + column % rows
    hits = tile_labels[:, None] == column[None, :]
    part, slopes = pair_block(tile_images, tile_texts, hits, temper, offset)
    image_part = temper * jnp.dot(slopes, tile_texts, preferred_element_type=jnp.float32)
    text_part = temper * jnp.dot(slopes.T, tile_images, preferred_element_type=jnp.float32)
    image_sum = lax.psum_scatter(image_part, "blk", scatter_dimension=0, tiled=True, axis_index_groups=across_groups)
    text_sum = lax.psum_scatter(text_part, "blk", scatter_dimension=0, tiled=True, axis_index_groups=down_groups)

    every_grad = lax.all_gather(text_sum, "group", axis=0, tiled=True)
    source = jnp.argmax((partner == group_place).astype(jnp.int32))
    text_home = lax.dynamic_slice_in_dim(every_grad, source * rows, rows, 0)
    total = lax.psum(part, ("blk", "group"))
    loss = total / (group_count * rows * cycle_size * cycle_size)
    return (image_sum[None], text_home[None], jnp.reshape(loss, (1,)))


def solution(mesh):
    in_specs = (P("group", "blk", None), P("group", "blk", None), P("group", "blk"), P(), P(), P())
    out_specs = (P("group", "blk", None), P("group", "blk", None), P())
    return jax.shard_map(shards, mesh=mesh, in_specs=in_specs, out_specs=out_specs, check_vma=False)
```

time: 1120 us -> 310 us (0.28)
  waiting for transfers between devices: 686 us -> 168 us
  matrix products: 195 us -> 15.3 us
  blocking collectives: 148 us -> 98.8 us
  loops' own time: 45.2 us -> 0 us
  starting transfers between devices: 14.4 us -> 0.2 us
    ppermute x192 -> x0, waiting for transfers between devices: 685 us -> none  [shifted(): lax.ppermute(array, axis, [(i, (i + by) % size) for i in range(size)])]
    dot_general x64 -> x1, matrix products: 96.4 us -> 5.85 us  [pair_block(): jnp.dot(images, texts.T, preferred_element_type=jnp.float32)]
    dot_general x128 -> x2, matrix products: 98.9 us -> 9.41 us  [the longest x1 5.43 us: shards(): jnp.dot(slopes, tile_texts, preferred_element_type=jnp.float32)]
    all_gather x0 -> x3, waiting for transfers between devices: none -> 84.5 us  [the longest x1 60.9 us: shards(): lax.all_gather(images, 'blk', axis=0, tiled=True, axis_index_groups=acros...]
    reduce_scatter x1 -> x2, waiting for transfers between devices: 0.02 us -> 82.3 us  [the longest x1 48.1 us: shards(): lax.psum_scatter(text_part, 'blk', scatter_dimension=0, tiled=True, axis_...]
    psum x1, blocking collectives: 137 us -> 77.7 us  [shards(): total = lax.psum(part, ('blk', 'group'))]
    another operation x1 -> x0, loops' own time: 45.2 us -> none  [shards(): finished = lax.fori_loop(0, cycle_size, advance, start)]
    ppermute x192 -> x0, starting transfers between devices: 14.4 us -> none  [shifted(): lax.ppermute(array, axis, [(i, (i + by) % size) for i in range(size)])]
  transfers between devices with their start and end apart: 193 -> 5, of which waited for: 192 -> 4; matrix products, arithmetic and copies ran while one was open for 18% -> 3% of each run, Pallas kernels for 0% -> 0%
where the time goes in v1:
time: 310 us; the launch traced here: 309 us
  waiting for transfers between devices  168 us (54%)
  blocking collectives  98.8 us (32%)
  between operations  18.8 us (6%)
  matrix products  15.3 us (5%)
  local copies, waits for them, and re-layouts  7.86 us (3%)
    psum x1, blocking collectives, shards(): total = lax.psum(part, ('blk', 'group'))  77.7 us
    all_gather x1, waiting for transfers between devices, shards(): lax.all_gather(images, 'blk', axis=0, tiled=True, axis_index_groups=acros...  60.9 us
    reduce_scatter x1, waiting for transfers between devices, shards(): lax.psum_scatter(text_part, 'blk', scatter_dimension=0, tiled=True, axis_...  48.1 us
    reduce_scatter x1, waiting for transfers between devices, shards(): lax.psum_scatter(image_part, 'blk', scatter_dimension=0, tiled=True, axis...  34.2 us
    all_gather x1, waiting for transfers between devices, shards(): lax.all_gather(partner_block, 'blk', axis=0, tiled=True, axis_index_group...  23.6 us
    all_gather x1, blocking collectives, shards(): every_text = lax.all_gather(own_texts, 'group', axis=0, tiled=True)  10.8 us
    unnamed x1, blocking collectives  10.4 us
  transfers between devices with their start and end apart: 5, of which 4 were waited for; matrix products, arithmetic and copies ran while one was open for 3% of the time, Pallas kernels for 0%

profile of v1, /device:TPU:1, one launch (start us, length us, event | category | flops | bytes accessed | tf_op | source)
XLA Modules:
  0.0 309.2 jit_solution(4616922460364439062)
XLA Ops:
  7.2 0.0 all-gather.12.cloned.1.call-start
  7.2 1.2 dynamic_slice.9
  9.1 10.8 %all-gather = bf16[1,384,1152]{2,1,0:T(8,128)(2,1)S(1)} all-gather(bf16[1,96,1152]{2,1,0:T(8,128)(2,1)} %param.7), channel_id=2, replica_groups=mesh['blk'=64,'group'=4] {'group'}, dimensions={1}, use_global_device_ids=true | all-gather | bytes 1105920 | tf_op jit(solution)/shard_map/all_gather | solution.py:33
  19.9 0.7 constant_dynamic-slice_fusion
  20.6 0.0 all-gather.10.cloned.1.call-start
  20.7 0.7 all-gather.10.cloned.1.call-update
  21.4 0.0 reduce-scatter.5.cloned.1.call-start
  22.8 1.3 dynamic-slice.1
  24.7 0.8 bitcast_dynamic-update-slice_fusion
  25.5 10.4 %all-reduce = s32[768]{0:T(1024)S(1)} all-reduce(s32[768]{0:T(1024)S(1)} %bitcast_dynamic-update-slice_fusion), channel_id=4, replica_groups={{0,4,8,12,16,20,24,28},{32,36,40,44,48,52,56,60},{64,68,72,76,80,84,88,..., use_global_device_ids=true, to_apply=%add | all-reduce | flops 768 | bytes 6144
  35.9 23.6 %all-gather.12.cloned.1.call-done = bf16[1,768,1152]{2,1,0:T(8,128)(2,1)} async-done(((bf16[1,96,1152]{2,1,0:T(8,128)(2,1)}), bf16[1,768,1152]{2,1,0:T(8,128)(2,1)}) %all-gather.12.cloned.1.call-update) | async-done | bytes 1769488 | tf_op jit(solution)/shard_map/all_gather | solution.py:39
  59.5 60.9 %all-gather.10.cloned.1.call-done = bf16[1,768,1152]{2,1,0:T(8,128)(2,1)} async-done(((bf16[1,96,1152]{2,1,0:T(8,128)(2,1)}), bf16[1,768,1152]{2,1,0:T(8,128)(2,1)}) %all-gather.10.cloned.1.call-update) | async-done | bytes 1769488 | tf_op jit(solution)/shard_map/all_gather | solution.py:37
  120.3 5.8 %fusion.3 = (f32[]{:T(128)}, f32[768,768]{1,0:T(8,128)S(1)}) fusion(s32[768]{0:T(1024)S(1)} %all-reduce, f32[]{:T(128)} %bitcast.52, f32[]{:T(128)} %bitcast, s32[768]{0:T(1024)S(1)} %fusion.25, bf16[1,768,1152]{2,1,0:T(8,128)(2,1)} %all-gather.10.cloned.1.call-done, bf16[1,768,1152]{2,1,0:T(8,128)(2,1)} %all-gather.12.cloned.1.call-done), kind=kOutput, calls=%fused_computation.8 | convolution fusion | flops 1366032384 | bytes 5904396 | tf_op jit(solution)/shard_map/dot_general | solution.py:10
  126.2 1.4 copy-done.3
  127.6 4.0 %convolution_multiply_fusion = f32[768,1152]{1,0:T(8,128)} fusion(bf16[1,768,1152]{2,1,0:T(8,128)(2,1)S(1)} %copy-done.2, f32[]{:T(128)} %bitcast, f32[768,768]{1,0:T(8,128)S(1)} %get-tuple-element.6, s32[768]{0:T(1024)S(1)} %all-reduce, f32[]{:T(128)} %bitcast.53, s32[768]{0:T(1024)S(1)} %fusion.25), kind=kOutput, calls=%fused_computation.1 | convolution fusion | flops 1365147648 | bytes 7673864 | tf_op jit(solution)/shard_map/dot_general | solution.py:46
  131.6 0.0 all-gather.8.cloned.1.call-start
  131.7 48.1 %reduce-scatter.5.cloned.1.call-done = f32[96,1152]{1,0:T(8,128)} async-done(((f32[768,1152]{1,0:T(8,128)}), f32[96,1152]{1,0:T(8,128)}) %reduce-scatter.5.cloned.1.call-update) | async-done | bytes 442384 | tf_op jit(solution)/shard_map/reduce_scatter | solution.py:48
  179.8 0.0 reduce-scatter.3.cloned.1.call-start
  179.8 5.4 %convolution_multiply_fusion.1 = f32[768,1152]{1,0:T(8,128)} fusion(bf16[1,768,1152]{2,1,0:T(8,128)(2,1)S(1)} %copy-done.1, f32[]{:T(128)} %bitcast, f32[768,768]{1,0:T(8,128)} %copy-done.3, s32[768]{0:T(1024)S(1)} %all-reduce, f32[]{:T(128)} %bitcast.51, s32[768]{0:T(1024)S(1)} %fusion.25), kind=kOutput, calls=%fused_computation.2 | convolution fusion | flops 1365147648 | bytes 7673864 | tf_op jit(solution)/shard_map/dot_general | solution.py:45
  185.3 0.6 copy-done
  185.9 0.6 fusion.27
  187.1 77.7 %psum.7 = f32[]{:T(128)} all-reduce(f32[]{:T(128)} %get-tuple-element.5), channel_id=1, replica_groups=mesh['blk'=64,'group'=4] {'blk','group'}, use_global_device_ids=true, to_apply=%region_4.5 | all-reduce | flops 1 | bytes 8 | tf_op jit(solution)/shard_map/psum | solution.py:53
  265.5 1.8 dynamic-slice_bitcast_fusion
  267.3 34.2 %reduce-scatter.3.cloned.1.call-done = f32[96,1152]{1,0:T(8,128)} async-done(((f32[768,1152]{1,0:T(8,128)}), f32[96,1152]{1,0:T(8,128)}) %reduce-scatter.3.cloned.1.call-update) | async-done | bytes 442384 | tf_op jit(solution)/shard_map/reduce_scatter | solution.py:47
  (13 shorter events, 0.1 us)
Async XLA Ops:
  7.2 52.3 %all-gather.12.cloned.1.call-start = ((), (), s32[]{:S(2)}) async-start(), calls=%async_computation.6 | async-start | bytes 1990656 | tf_op jit(solution)/shard_map/all_gather | solution.py:39
  20.6 99.7 %all-gather.10.cloned.1.call-start = ((), (), s32[]{:S(2)}) async-start(), calls=%async_computation.5 | async-start | bytes 1990656 | tf_op jit(solution)/shard_map/all_gather | solution.py:37
  21.4 158.4 %reduce-scatter.5.cloned.1.call-start = ((), (), s32[]{:S(2)}) async-start(), calls=%async_computation.3 | async-start | bytes 3981312 | tf_op jit(solution)/shard_map/reduce_scatter | solution.py:48
  120.3 7.3 %copy-start.2 = (bf16[1,768,1152]{2,1,0:T(8,128)(2,1)S(1)}, bf16[1,768,1152]{2,1,0:T(8,128)(2,1)}, u32[]{:S(2)}) copy-start(bf16[1,768,1152]{2,1,0:T(8,128)(2,1)} %all-gather.10.cloned.1.call-done) | copy-start | bytes 5308420
  126.2 1.4 copy-start.3
  131.6 48.2 %copy-start.1 = (bf16[1,768,1152]{2,1,0:T(8,128)(2,1)S(1)}, bf16[1,768,1152]{2,1,0:T(8,128)(2,1)}, u32[]{:S(2)}) copy-start(bf16[1,768,1152]{2,1,0:T(8,128)(2,1)} %all-gather.12.cloned.1.call-done) | copy-start | bytes 5308420
  131.6 133.8 %all-gather.8.cloned.1.call-start = ((), (), s32[]{:S(2)}) async-start(), calls=%async_computation.4 | async-start | bytes 2211840 | tf_op jit(solution)/shard_map/all_gather | solution.py:50
  179.8 121.7 %reduce-scatter.3.cloned.1.call-start = ((), (), s32[]{:S(2)}) async-start(), calls=%async_computation.2 | async-start | bytes 3981312 | tf_op jit(solution)/shard_map/reduce_scatter | solution.py:47
  185.3 0.7 copy-start
Sparse Core Ops, SparseCore 0:
  20.8 38.6 all-gather.11
  62.1 58.2 all-gather.9
  131.7 47.9 reduce-scatter.4
  181.6 29.1 all-gather.7
  215.9 85.5 reduce-scatter.2

commit v2 on v1

v2 whole, which is shorter than its diff:
```python
import functools

import jax
import jax.numpy as jnp
from jax import lax
from jax.experimental import pallas as pl
from jax.experimental.pallas import tpu as pltpu
from jax.sharding import PartitionSpec as P

NZ, NX, NY = 8, 4, 4
LANES = 128
SCALE_ROWS = 16
TOP = 14.9657842846620869


def kernel(total_pairs, partner_ref, temp_ref, bias_ref, img_ref, txt_ref, lab_in_ref,
           img_out, txt_out, loss_out,
           ibuf, tbuf, xbuf, labrow, labcol, slopes, slopes_t, gi, gt, tsum, loss_acc, loss_in,
           zq_out, zq_in, yq_out, yq_in, sq_out, sq_in, xq_out, xq_in,
           send_sems, recv_sems):
    rows, width = img_ref.shape[1], img_ref.shape[2]
    half = rows // 2
    tiles = width // LANES
    blk, group = lax.axis_index("blk"), lax.axis_index("group")
    z, x_hi, y = blk // (NX // 2 * NY), (blk // NY) % (NX // 2), blk % NY
    x_lo, core = group // 2, group % 2
    x = x_hi * 2 + x_lo

    def device(z_at, x_at, y_at, core_at):
        return (z_at * (NX // 2 * NY) + (x_at // 2) * NY + y_at, (x_at % 2) * 2 + core_at)

    def flipped(value, bit):
        return value + bit - 2 * bit * ((value // bit) % 2)

    z_up, z_down = device((z + 1) % NZ, x, y, core), device((z + NZ - 1) % NZ, x, y, core)
    y_up, y_down = device(z, x, (y + 1) % NY, core), device(z, x, (y + NY - 1) % NY, core)
    x_up, x_down = device(z, (x + 1) % NX, y, core), device(z, (x + NX - 1) % NX, y, core)
    twin = device(z, x, y, 1 - core)
    loss_peers = [twin, device(flipped(z, 1), x, y, core), device(flipped(z, 2), x, y, core),
                  device(flipped(z, 4), x, y, core), device(z, flipped(x, 1), y, core),
                  device(z, flipped(x, 2), y, core), device(z, x, flipped(y, 1), core),
                  device(z, x, flipped(y, 2), core)]

    greeted = [z_up, z_down, y_up, y_down, x_up, x_down, twin,
               loss_peers[2], loss_peers[3], loss_peers[5], loss_peers[7]]
    barrier = pltpu.get_barrier_semaphore()
    for peer in greeted:
        pl.semaphore_signal(barrier, inc=1, device_id=peer, device_id_type=pl.DeviceIdType.MESH)
    pl.semaphore_wait(barrier, len(greeted))

    places, pending = {}, []

    def copy_of(name, src, dst, peer):
        place = places.setdefault(name, len(places))
        return pltpu.make_async_remote_copy(
            src_ref=src, dst_ref=dst, send_sem=send_sems.at[place], recv_sem=recv_sems.at[place],
            device_id=peer, device_id_type=pl.DeviceIdType.MESH)

    def send(name, src, dst, peer):
        copy = copy_of(name, src, dst, peer)
        copy.start()
        pending.append(copy)

    def arrived(name, dst, peer):
        copy_of(name, dst, dst, peer).wait_recv()

    A, B = 0, 1

    def part(chunk):
        return pl.ds(chunk * half, half)

    def image_slot(rel, chunk):
        return ibuf.at[pl.ds((rel % NZ) * rows + chunk * half, half)]

    def text_slot(rel, p, chunk):
        return tbuf.at[pl.ds(((rel % NY) * 2 + p) * rows + chunk * half, half)]

    def x_slot(side, rel, chunk):
        return xbuf.at[side, rel % NX, part(chunk)]

    labrow[0] = jnp.zeros((8, LANES), jnp.int32)
    labrow[0, 0:1, 0:rows] = lab_in_ref[...]

    def z_send(hop, way, chunk):
        src = img_ref.at[0, part(chunk)] if hop == 1 else image_slot(-way * (hop - 1), chunk)
        send(("z", hop, way, chunk), src, image_slot(-way * hop, chunk), z_up if way > 0 else z_down)
        if chunk == (A if way > 0 else B) and (way > 0 or hop < NZ // 2):
            send(("label", hop, way), labrow.at[(-way * (hop - 1)) % NZ], labrow.at[(-way * hop) % NZ],
                 z_up if way > 0 else z_down)

    def z_arrived(hop, way, chunk):
        arrived(("z", hop, way, chunk), image_slot(-way * hop, chunk), z_up)
        if chunk == (A if way > 0 else B) and (way > 0 or hop < NZ // 2):
            arrived(("label", hop, way), labrow.at[(-way * hop) % NZ], z_up)

    def x_send(hop, way, chunk):
        src = txt_ref.at[0, part(chunk)] if hop == 1 else x_slot(0, -way * (hop - 1), chunk)
        send(("x", hop, way, chunk), src, x_slot(0, -way * hop, chunk), x_up if way > 0 else x_down)

    def x_arrived(hop, way, chunk):
        arrived(("x", hop, way, chunk), x_slot(0, -way * hop, chunk), x_up)

    def twin_send(rel, chunk):
        src = txt_ref.at[0, part(chunk)] if rel == 0 else x_slot(0, rel, chunk)
        send(("twin", rel, chunk), src, x_slot(1, rel, chunk), twin)

    def twin_arrived(rel, chunk):
        arrived(("twin", rel, chunk), x_slot(1, rel, chunk), twin)

    def y_send(hop, way, p, chunk):
        send(("y", hop, way, p, chunk), text_slot(-way * (hop - 1), p, chunk), text_slot(-way * hop, p, chunk),
             y_up if way > 0 else y_down)

    def y_arrived(hop, way, p, chunk):
        arrived(("y", hop, way, p, chunk), text_slot(-way * hop, p, chunk), y_up)

    target = partner_ref[group]
    same_side = target // 2 == x_lo
    same_core = target % 2 == core
    near = 1 + 2 * x_lo
    far = 3 - 2 * x_lo

    def choose(p, chunk):
        middle = [txt_ref[0, part(chunk)] if p == 0 else xbuf[0, 2, part(chunk)], xbuf[1, 2 * p, part(chunk)]]
        side_at = near if p == 0 else far
        side = [xbuf[0, side_at, part(chunk)], xbuf[1, side_at, part(chunk)]]
        middle = jnp.where(same_core, middle[0], middle[1])
        side = jnp.where(same_core, side[0], side[1])
        tbuf[pl.ds(p * rows + chunk * half, half), :] = jnp.where(same_side, middle, side)

    z_send(1, 1, A)
    x_send(1, 1, A)
    z_send(1, -1, B)
    x_send(1, -1, B)
    twin_send(0, A)
    twin_send(0, B)
    z_send(1, 1, B)
    z_send(1, -1, A)
    x_send(1, 1, B)
    x_send(1, -1, A)
    ibuf[0:rows, :] = img_ref[0]

    x_arrived(1, 1, A)
    x_send(2, 1, A)
    twin_send(3, A)
    x_arrived(1, -1, B)
    x_send(2, -1, B)
    twin_send(1, B)
    z_arrived(1, 1, A)
    z_send(2, 1, A)
    z_arrived(1, -1, B)
    z_send(2, -1, B)
    x_arrived(1, 1, B)
    twin_send(3, B)
    x_arrived(1, -1, A)
    twin_send(1, A)
    z_arrived(1, 1, B)
    z_send(2, 1, B)
    z_arrived(1, -1, A)
    z_send(2, -1, A)
    for chunk in (A, B):
        for rel in (0, 1, 3):
            twin_arrived(rel, chunk)
        choose(0, chunk)
        y_send(1, 1, 0, chunk)
        y_send(1, -1, 0, chunk)
    x_arrived(2, 1, A)
    twin_send(2, A)
    x_arrived(2, -1, B)
    twin_send(2, B)
    for chunk in (A, B):
        twin_arrived(2, chunk)
        choose(1, chunk)
        y_send(1, 1, 1, chunk)
        y_send(1, -1, 1, chunk)
    z_arrived(2, 1, A)
    z_send(3, 1, A)
    z_arrived(2, -1, B)
    z_send(3, -1, B)
    y_arrived(1, 1, 0, A)
    y_send(2, 1, 0, A)
    z_arrived(2, 1, B)
    z_send(3, 1, B)
    z_arrived(2, -1, A)
    z_send(3, -1, A)
    y_arrived(1, -1, 0, A)
    y_arrived(1, -1, 0, B)
    y_send(2, -1, 0, B)
    y_arrived(1, 1, 0, B)
    z_arrived(3, 1, A)
    z_send(4, 1, A)
    z_arrived(3, -1, B)
    z_send(4, -1, B)
    y_arrived(1, 1, 1, A)
    y_send(2, 1, 1, A)
    y_arrived(1, -1, 1, A)
    y_arrived(1, -1, 1, B)
    y_send(2, -1, 1, B)
    y_arrived(1, 1, 1, B)
    z_arrived(3, 1, B)
    z_arrived(3, -1, A)
    z_arrived(4, 1, A)
    z_arrived(4, -1, B)
    for p in (0, 1):
        y_arrived(2, 1, p, A)
        y_arrived(2, -1, p, B)

    temper = jnp.exp(jnp.full((1, LANES), temp_ref[0], jnp.float32))
    offset = jnp.full((1, LANES), bias_ref[0], jnp.float32)
    for rel in range(NZ):
        column = jnp.broadcast_to(labrow[rel, 0:1, :], (LANES, LANES)).T
        labcol[rel * rows:(rel + 1) * rows, :] = column[:rows]
    n_i, n_t = NZ * rows, 2 * NY * rows
    wide = 2 * LANES
    loss_acc[0] = jnp.zeros((8, LANES), jnp.float32)

    def slope_tile(step, carry):
        top = pl.multiple_of(step * wide, wide)
        images = ibuf[pl.ds(top, wide), :]
        for left in range(0, n_t, wide):
            dots = lax.dot_general(images, tbuf[left:left + wide, :], (((1,), (1,)), ((), ())),
                                   preferred_element_type=jnp.float32)
            for at in range(0, wide, LANES):
                logits = temper * dots[:, at:at + LANES] + offset
                column = lax.broadcasted_iota(jnp.int32, (1, LANES), 1) + (left + at)
                own = column + ((z * (NX // 2) + x_hi) * NY + y) * rows
                for b in range(1, 2 * NY):
                    owner = (z * (NX // 2) + (x_hi + b % 2) % 2) * NY + (y + b // 2) % NY
                    own = jnp.where(column >= b * rows, column + (owner - b) * rows, own)
                hit = labcol[pl.ds(top, wide), :] == own
                margin = jnp.where(hit, -logits, logits)
                small = jnp.exp(-jnp.abs(logits))
                base = 1.0 + small
                inverse = 1.0 / base
                log_part = jnp.log(base) + (small - (base - 1.0)) * inverse
                loss = jnp.maximum(margin, 0.0) + log_part
                loss_acc[0] += jnp.sum(loss.reshape(wide // 8, 8, LANES), axis=0)
                slope = jnp.where(margin >= 0.0, 1.0, small) * inverse
                slope = jnp.where(hit, -slope, slope).astype(jnp.bfloat16)
                slopes[pl.ds(top, wide), left + at:left + at + LANES] = slope
                slopes_t[left + at:left + at + LANES, pl.ds(top, wide)] = slope.T
        return carry

    lax.fori_loop(0, n_i // wide, slope_tile, 0)

    def grad_images(first, count):
        gi[first * rows:(first + count) * rows, :] = jnp.dot(
            slopes[first * rows:(first + count) * rows, :], tbuf[...], preferred_element_type=jnp.float32)

    def grad_texts(first, count):
        gt[first * rows:(first + count) * rows, :] = jnp.dot(
            slopes_t[first * rows:(first + count) * rows, :], ibuf[...], preferred_element_type=jnp.float32)

    def packed(out, value):
        tops = jnp.max(jnp.abs(value).reshape(half // SCALE_ROWS, SCALE_ROWS, width), axis=0)
        top = tops[:, 0:LANES]
        for t in range(1, tiles):
            top = jnp.maximum(top, tops[:, t * LANES:(t + 1) * LANES])
        exponent = jnp.ceil(jnp.log2(jnp.maximum(top, 1e-30)))
        inverse = jnp.concatenate([jnp.exp2(TOP - exponent)] * (half // SCALE_ROWS), axis=0)
        out[tiles * half:tiles * half + SCALE_ROWS, :] = exponent.astype(jnp.int16)
        for t in range(tiles):
            scaled = jnp.round(value[:, t * LANES:(t + 1) * LANES] * inverse)
            out[t * half:(t + 1) * half, :] = scaled.astype(jnp.int32).astype(jnp.int16)

    def unpacked(message):
        exponent = message[tiles * half:tiles * half + SCALE_ROWS, :].astype(jnp.int32).astype(jnp.float32)
        scale = jnp.concatenate([jnp.exp2(exponent - TOP)] * (half // SCALE_ROWS), axis=0)
        return jnp.concatenate(
            [message[t * half:(t + 1) * half, :].astype(jnp.int32).astype(jnp.float32) * scale for t in range(tiles)],
            axis=1)

    def ring(kind, n, out, inbox, up, down, partial):
        halfway = n // 2

        def slot(hop, way, chunk):
            return (0 if way > 0 else 1), 2 * (hop - 1) + chunk

        def get(hop, way, chunk):
            box = inbox.at[slot(hop, way, chunk)]
            arrived((kind, hop, way, chunk), box, up)
            return unpacked(box)

        def put(hop, way, chunk):
            value = partial(way * (halfway + 1 - hop), chunk)
            fresh = hop == 1 or (hop == 2 and chunk == (B if way > 0 else A))
            if not fresh:
                value = value + get(hop - 1, way, chunk)
            at = slot(hop, way, chunk)
            packed(out.at[at], value)
            send((kind, hop, way, chunk), out.at[at], inbox.at[at], up if way > 0 else down)

        def last(chunk):
            return partial(0, chunk) + get(halfway, 1, chunk) + get(halfway, -1, chunk)

        return put, last

    z_put, z_last = ring(
        "gz", NZ, zq_out, zq_in, z_up, z_down,
        lambda rel, chunk: gi[(rel % NZ) * rows + chunk * half:(rel % NZ) * rows + (chunk + 1) * half, :])
    y_puts, y_lasts = [], []
    for p in (0, 1):
        put, last = ring(
            ("gy", p), NY, yq_out.at[p], yq_in.at[p], y_up, y_down,
            lambda rel, chunk, p=p: gt[((rel % NY) * 2 + p) * rows + chunk * half:
                                       ((rel % NY) * 2 + p) * rows + (chunk + 1) * half, :])
        y_puts.append(put)
        y_lasts.append(last)

    def loss_step(step):
        send(("loss", step), loss_acc.at[step], loss_in.at[step], loss_peers[step])
        arrived(("loss", step), loss_in.at[step], twin)
        loss_acc[step + 1] = loss_acc[step] + loss_in[step]

    grad_images(3, 3)
    z_put(1, 1, A)
    z_put(1, -1, B)
    grad_texts(4, 2)
    y_puts[1](1, 1, A)
    y_puts[1](1, -1, B)
    z_put(2, 1, B)
    z_put(2, -1, A)
    y_puts[0](1, 1, A)
    y_puts[0](1, -1, B)
    grad_texts(2, 2)
    grad_texts(6, 2)
    y_puts[1](2, 1, B)
    y_puts[1](2, -1, A)
    z_put(2, 1, A)
    z_put(2, -1, B)
    y_puts[0](2, 1, B)
    y_puts[0](2, -1, A)
    y_puts[1](2, 1, A)
    y_puts[1](2, -1, B)
    grad_images(0, 3)
    grad_images(6, 2)
    grad_texts(0, 2)
    z_put(3, 1, B)
    z_put(3, -1, A)
    loss_step(0)
    y_puts[0](2, 1, A)
    y_puts[0](2, -1, B)
    z_put(3, 1, A)
    z_put(3, -1, B)
    loss_step(1)

    def twin_grad_send(p, chunk):
        packed(sq_out.at[p, chunk], tsum[p, part(chunk)])
        send(("gs", p, chunk), sq_out.at[p, chunk], sq_in.at[p, chunk], twin)

    def y_finish(p, chunk):
        tsum[p, part(chunk)] = y_lasts[p](chunk)
        twin_grad_send(p, chunk)

    twin_group = x_lo * 2 + (1 - core)
    twin_target = partner_ref[twin_group]
    across = (1 - x_lo) * 2 + core

    def weight(who, home):
        return jnp.full((1, LANES), jnp.where(who == home, 1.0, 0.0), jnp.float32)

    weights = {0: (weight(target, group), weight(twin_target, group)),
               1: (weight(target, across), weight(twin_target, across))}

    def x_partial(rel, chunk):
        rel = rel % NX
        p = {0: 0, 2: 1, 1: x_lo, 3: 1 - x_lo}[rel]
        own_weight, twin_weight = weights[rel % 2]
        own, other = tsum[p, part(chunk)], unpacked(sq_in.at[p, chunk])
        return jnp.concatenate(
            [own[:, t * LANES:(t + 1) * LANES] * own_weight + other[:, t * LANES:(t + 1) * LANES] * twin_weight
             for t in range(tiles)], axis=1)

    x_put, x_last = ring("gx", NX, xq_out, xq_in, x_up, x_down, x_partial)

    y_finish(1, A)
    y_finish(1, B)
    z_put(4, 1, B)
    z_put(4, -1, A)
    loss_step(2)
    for chunk in (A, B):
        arrived(("gs", 1, chunk), sq_in.at[1, chunk], twin)
    x_put(1, 1, A)
    x_put(1, -1, B)
    loss_step(3)
    y_finish(0, A)
    y_finish(0, B)
    z_put(4, 1, A)
    z_put(4, -1, B)
    loss_step(4)
    for chunk in (A, B):
        arrived(("gs", 0, chunk), sq_in.at[0, chunk], twin)
    x_put(2, 1, B)
    x_put(2, -1, A)
    loss_step(5)
    x_put(2, 1, A)
    x_put(2, -1, B)
    loss_step(6)
    loss_step(7)
    loss_out[0] = jnp.sum(loss_acc[8]) / total_pairs

    def write(out, chunk, value):
        for t in range(tiles):
            out[0, part(chunk), t * LANES:(t + 1) * LANES] = temper * value[:, t * LANES:(t + 1) * LANES]

    for chunk in (A, B):
        write(img_out, chunk, z_last(chunk))
    for chunk in (A, B):
        write(txt_out, chunk, x_last(chunk))
    for copy in pending:
        copy.wait_send()


def shards(image_embeds, text_embeds, positives, partner, log_temp, bias):
    _, rows, width = image_embeds.shape
    half, tiles = rows // 2, width // LANES
    message = (tiles * half + SCALE_ROWS, LANES)
    n_i, n_t = NZ * rows, 2 * NY * rows
    cycle, groups = lax.axis_size("blk"), lax.axis_size("group")
    total_pairs = groups * rows * cycle * cycle
    vmem = pl.BlockSpec(memory_space=pltpu.VMEM)
    smem = pl.BlockSpec(memory_space=pltpu.SMEM)
    f32, bf16, i16, i32 = jnp.float32, jnp.bfloat16, jnp.int16, jnp.int32
    copies = 160
    return pl.pallas_call(
        functools.partial(kernel, float(total_pairs)),
        out_shape=(jax.ShapeDtypeStruct((1, rows, width), f32), jax.ShapeDtypeStruct((1, rows, width), f32),
                   jax.ShapeDtypeStruct((1,), f32)),
        in_specs=[smem, smem, smem, vmem, vmem, vmem],
        out_specs=(vmem, vmem, smem),
        scratch_shapes=[
            pltpu.VMEM((n_i, width), bf16),
            pltpu.VMEM((n_t, width), bf16),
            pltpu.VMEM((2, NX, rows, width), bf16),
            pltpu.VMEM((NZ, 8, LANES), i32),
            pltpu.VMEM((n_i, LANES), i32),
            pltpu.VMEM((n_i, n_t), bf16),
            pltpu.VMEM((n_t, n_i), bf16),
            pltpu.VMEM((n_i, width), f32),
            pltpu.VMEM((n_t, width), f32),
            pltpu.VMEM((2, rows, width), f32),
            pltpu.VMEM((9, 8, LANES), f32),
            pltpu.VMEM((8, 8, LANES), f32),
            pltpu.VMEM((2, NZ, *message), i16),
            pltpu.VMEM((2, NZ, *message), i16),
            pltpu.VMEM((2, 2, NY, *message), i16),
            pltpu.VMEM((2, 2, NY, *message), i16),
            pltpu.VMEM((2, 2, *message), i16),
            pltpu.VMEM((2, 2, *message), i16),
            pltpu.VMEM((2, NX, *message), i16),
            pltpu.VMEM((2, NX, *message), i16),
            pltpu.SemaphoreType.DMA((copies,)),
            pltpu.SemaphoreType.DMA((copies,)),
        ],
        compiler_params=pltpu.CompilerParams(
            collective_id=0, has_side_effects=True, vmem_limit_bytes=48 * 1024 * 1024),
    )(partner, log_temp, bias, image_embeds, text_embeds, positives)


def solution(mesh):
    in_specs = (P("group", "blk", None), P("group", "blk", None), P("group", "blk"), P(), P(), P())
    out_specs = (P("group", "blk", None), P("group", "blk", None), P())
    return jax.shard_map(shards, mesh=mesh, in_specs=in_specs, out_specs=out_specs, check_vma=False)
```

time: 310 us -> 91.7 us (0.30)
  the two profiles are of different devices: /device:TPU:1 before, /device:TPU:32 now
where the time goes in v2:
time: 91.7 us; the launch traced here: 91.6 us
  Pallas kernels  84.4 us (92%)
  between operations  3.74 us (4%)
  local copies, waits for them, and re-layouts  3.4 us (4%)
    pallas_call x1, Pallas kernels, shards(): pl.pallas_call(functools.partial(kernel, float(total_pairs)), out_shape=(...  84.4 us
    unnamed x10, local copies, waits for them, and re-layouts  3.4 us

profile of v2, /device:TPU:32, one launch (start us, length us, event | category | flops | bytes accessed | tf_op | source)
XLA Modules:
  0.0 91.6 jit_solution(9247291247923825848)
XLA Ops:
  1.3 0.0 copy-start.2
  1.3 0.0 copy-start.3
  2.0 0.0 copy-done.2
  2.0 0.0 copy-done.3
  2.0 0.0 copy-start
  2.0 0.9 %copy-done = bf16[1,96,1152]{2,1,0:T(8,128)(2,1)S(1)} copy-done((bf16[1,96,1152]{2,1,0:T(8,128)(2,1)S(1)}, bf16[1,96,1152]{2,1,0:T(8,128)(2,1)}, u32[]{:S(2)}) %copy-start) | copy-done | bytes 221208
  2.9 0.0 copy-start.1
  2.9 0.9 %copy-done.1 = bf16[1,96,1152]{2,1,0:T(8,128)(2,1)S(1)} copy-done((bf16[1,96,1152]{2,1,0:T(8,128)(2,1)S(1)}, bf16[1,96,1152]{2,1,0:T(8,128)(2,1)}, u32[]{:S(2)}) %copy-start.1) | copy-done | bytes 221208
  3.9 84.4 %shard_map.85 = (f32[1,96,1152]{2,1,0:T(8,128)S(1)}, f32[1,96,1152]{2,1,0:T(8,128)S(1)}, f32[1]{0:T(128)}) custom-call(s32[4]{0:T(128)S(1)} %copy-done.2, f32[1]{0:T(128)S(6)} %copy.12.temp_ref, f32[1]{0:T(128)S(6)} %copy.13.bias_ref, bf16[1,96,1152]{2,1,0:T(8,128)(2,1)S(1)} %copy-done, bf16[1,96,1152]{2,1,0:T(8,128)(2,1)S(1)} %copy-done.1, ...), custom_call_target="tpu_custom_call" | custom-call | tf_op jit(solution)/shard_map/pallas_call | solution.py:425
  88.3 0.8 copy.14
  89.0 0.8 copy.15
Async XLA Ops:
  1.3 0.7 copy-start.2
  1.3 0.7 copy-start.3
  2.0 0.9 %copy-start = (bf16[1,96,1152]{2,1,0:T(8,128)(2,1)S(1)}, bf16[1,96,1152]{2,1,0:T(8,128)(2,1)}, u32[]{:S(2)}) copy-start(bf16[1,96,1152]{2,1,0:T(8,128)(2,1)} %img_ref.1) | copy-start | bytes 663556
  2.9 0.9 %copy-start.1 = (bf16[1,96,1152]{2,1,0:T(8,128)(2,1)S(1)}, bf16[1,96,1152]{2,1,0:T(8,128)(2,1)}, u32[]{:S(2)}) copy-start(bf16[1,96,1152]{2,1,0:T(8,128)(2,1)} %txt_ref.1) | copy-start | bytes 663556

commit v3 on v1

v3 whole, which is shorter than its diff:
```python
import functools

import jax
import jax.numpy as jnp
from jax import lax
from jax.experimental import pallas as pl
from jax.experimental.pallas import tpu as pltpu
from jax.sharding import PartitionSpec as P

NZ, NX, NY = 8, 4, 4
LANES = 128
SCALE_ROWS = 16
TOP = 14.9657842846620869


def kernel(total_pairs, partner_in, temp_in, bias_in, img_in, txt_in, lab_in,
           img_out, txt_out, loss_out,
           partner_ref, temp_ref, bias_ref, lab_own, ibuf, tbuf, xbuf, labrow, labcol, slopes, slopes_t, gi, gt, tsum,
           loss_acc, loss_in, zq_out, zq_in, yq_out, yq_in, sq_out, sq_in, xq_out, xq_in,
           send_sems, recv_sems, local_sems):
    rows, width = img_in.shape[1], img_in.shape[2]
    half = rows // 2
    tiles = width // LANES
    A, B = 0, 1
    OWN, NEAR, FAR, OPPOSITE = 0, 1, 2, 3

    local = [pltpu.make_async_copy(src, dst, local_sems.at[k]) for k, (src, dst) in enumerate((
        (txt_in.at[0], xbuf.at[0, OWN]), (img_in.at[0], ibuf.at[0:rows]), (lab_in, lab_own),
        (partner_in, partner_ref), (temp_in, temp_ref), (bias_in, bias_ref)))]
    for copy in local:
        copy.start()

    blk, group = lax.axis_index("blk"), lax.axis_index("group")
    z, x_hi, y = blk // (NX // 2 * NY), (blk // NY) % (NX // 2), blk % NY
    x_lo, core = group // 2, group % 2
    x = x_hi * 2 + x_lo

    def device(z_at, x_at, y_at, core_at):
        return ((z_at % NZ) * (NX // 2 * NY) + ((x_at % NX) // 2) * NY + y_at % NY, (x_at % 2) * 2 + core_at)

    z_up, z_down = device(z + 1, x, y, core), device(z + NZ - 1, x, y, core)
    y_up, y_down = device(z, x, y + 1, core), device(z, x, y + NY - 1, core)
    near, far = device(z, x + 1 + 2 * x_lo, y, core), device(z, x + 3 - 2 * x_lo, y, core)
    twin = device(z, x, y, 1 - core)
    x_others = [(d, device(z, x + d, y, core)) for d in range(1, NX)]
    y_others = [(d, device(z, x, y + d, core)) for d in range(1, NY)]
    z_others = [(d, device(z + d, x, y, core)) for d in range(1, NZ)]

    greeted = [twin] + [peer for _, peer in x_others + y_others + z_others]
    barrier = pltpu.get_barrier_semaphore()
    for peer in greeted:
        pl.semaphore_signal(barrier, inc=1, device_id=peer, device_id_type=pl.DeviceIdType.MESH)
    pl.semaphore_wait(barrier, len(greeted))

    places, pending = {}, []

    def copy_of(name, src, dst, peer):
        place = places.setdefault(name, len(places))
        return pltpu.make_async_remote_copy(
            src_ref=src, dst_ref=dst, send_sem=send_sems.at[place], recv_sem=recv_sems.at[place],
            device_id=peer, device_id_type=pl.DeviceIdType.MESH)

    def send(name, src, dst, peer):
        copy = copy_of(name, src, dst, peer)
        copy.start()
        pending.append(copy)

    def arrived(name, dst, peer):
        copy_of(name, dst, dst, peer).wait_recv()

    def part(chunk):
        return pl.ds(chunk * half, half)

    order = (0, 1, 7, 2, 6, 3, 5, 4)

    def image_at(rel, chunk=0):
        return order.index(rel % NZ) * rows + chunk * half

    def text_at(rel, p, chunk=0):
        return (p * NY + rel % NY) * rows + chunk * half

    def image_slot(rel, chunk):
        return ibuf.at[pl.ds(image_at(rel, chunk), half)]

    def text_slot(rel, p, chunk):
        return tbuf.at[pl.ds(text_at(rel, p, chunk), half)]

    def x_slot(side, which, chunk):
        return xbuf.at[side, which, part(chunk)]

    def z_send(hop, way, chunk):
        send(("z", hop, way, chunk), image_slot(-way * (hop - 1), chunk), image_slot(-way * hop, chunk),
             z_up if way > 0 else z_down)
        if chunk == (A if way > 0 else B) and (way > 0 or hop < NZ // 2):
            send(("label", hop, way), labrow.at[(-way * (hop - 1)) % NZ], labrow.at[(-way * hop) % NZ],
                 z_up if way > 0 else z_down)

    def z_arrived(hop, way, chunk):
        arrived(("z", hop, way, chunk), image_slot(-way * hop, chunk), z_up)
        if chunk == (A if way > 0 else B) and (way > 0 or hop < NZ // 2):
            arrived(("label", hop, way), labrow.at[(-way * hop) % NZ], z_up)

    def z_pass(hop, way, chunk):
        z_arrived(hop, way, chunk)
        if hop < NZ // 2 - 1 or (hop == NZ // 2 - 1 and chunk == (A if way > 0 else B)):
            z_send(hop + 1, way, chunk)

    def x_send(what, chunk):
        src, peer = {NEAR: (OWN, near), FAR: (OWN, far), OPPOSITE: (NEAR, far) if chunk == A else (FAR, near)}[what]
        send(("x", what, chunk), x_slot(0, src, chunk), x_slot(0, what, chunk), peer)

    def twin_send(what, chunk):
        send(("twin", what, chunk), x_slot(0, what, chunk), x_slot(1, what, chunk), twin)

    def x_pass(what, chunk):
        arrived(("x", what, chunk), x_slot(0, what, chunk), near)
        if what == (NEAR if chunk == A else FAR):
            x_send(OPPOSITE, chunk)
        twin_send(what, chunk)

    def y_send(hop, way, p, chunk):
        send(("y", hop, way, p, chunk), text_slot(-way * (hop - 1), p, chunk), text_slot(-way * hop, p, chunk),
             y_up if way > 0 else y_down)

    def y_pass(hop, way, p, chunk):
        arrived(("y", hop, way, p, chunk), text_slot(-way * hop, p, chunk), y_up)
        if hop == 1 and chunk == (A if way > 0 else B):
            y_send(2, way, p, chunk)

    def choose(p, chunk):
        target = partner_ref[group]
        same_side, same_core = target // 2 == x_lo, target % 2 == core
        here, there = (OWN, NEAR) if p == 0 else (OPPOSITE, FAR)
        for what in (here, there):
            arrived(("twin", what, chunk), x_slot(1, what, chunk), twin)
        here, there = (jnp.where(same_core, xbuf[0, what, part(chunk)], xbuf[1, what, part(chunk)])
                       for what in (here, there))
        tbuf[pl.ds(text_at(0, p, chunk), half), :] = jnp.where(same_side, here, there)
        y_send(1, 1, p, chunk)
        y_send(1, -1, p, chunk)

    local[0].wait()
    x_send(NEAR, A)
    x_send(FAR, A)
    local[1].wait()
    local[2].wait()
    labrow[0] = jnp.zeros((8, LANES), jnp.int32)
    labrow[0, 0:1, 0:rows] = lab_own[...]
    z_send(1, 1, A)
    z_send(1, -1, B)
    twin_send(OWN, A)
    twin_send(OWN, B)
    x_send(NEAR, B)
    x_send(FAR, B)
    z_send(1, 1, B)
    z_send(1, -1, A)
    for copy in local[3:]:
        copy.wait()

    temper = jnp.exp(jnp.full((1, LANES), temp_ref[0], jnp.float32))
    offset = jnp.full((1, LANES), bias_ref[0], jnp.float32)
    loss_acc[0] = jnp.zeros((8, LANES), jnp.float32)
    n_i, n_t = NZ * rows, 2 * NY * rows

    def label_columns(rels):
        for rel in rels:
            column = jnp.broadcast_to(labrow[rel, 0:1, :], (LANES, LANES)).T
            labcol[image_at(rel):image_at(rel) + rows, :] = column[:rows]

    def slope_quarter(i_half, p):
        left = p * NY * rows
        wide = NY * rows

        def step(k, carry):
            top = pl.multiple_of(i_half * (n_i // 2) + k * LANES, LANES)
            dots = lax.dot_general(ibuf[pl.ds(top, LANES), :], tbuf[left:left + wide, :], (((1,), (1,)), ((), ())),
                                   preferred_element_type=jnp.float32)
            for at in range(0, wide, LANES):
                logits = temper * dots[:, at:at + LANES] + offset
                column = lax.broadcasted_iota(jnp.int32, (1, LANES), 1) + at
                own = column + ((z * (NX // 2) + (x_hi + p) % 2) * NY + y) * rows
                for b in range(1, NY):
                    owner = (z * (NX // 2) + (x_hi + p) % 2) * NY + (y + b) % NY
                    own = jnp.where(column >= b * rows, column + (owner - b) * rows, own)
                hit = labcol[pl.ds(top, LANES), :] == own
                margin = jnp.where(hit, -logits, logits)
                small = jnp.exp(-jnp.abs(logits))
                base = 1.0 + small
                inverse = 1.0 / base
                log_part = jnp.log(base) + (small - (base - 1.0)) * inverse
                loss = jnp.maximum(margin, 0.0) + log_part
                loss_acc[0] += jnp.sum(loss.reshape(LANES // 8, 8, LANES), axis=0)
                slope = jnp.where(margin >= 0.0, 1.0, small) * inverse
                slope = jnp.where(hit, -slope, slope).astype(jnp.bfloat16)
                slopes[pl.ds(top, LANES), left + at:left + at + LANES] = slope
                slopes_t[left + at:left + at + LANES, pl.ds(top, LANES)] = slope.T
            return carry

        lax.fori_loop(0, n_i // 2 // LANES, step, 0)

    x_pass(NEAR, A)
    x_pass(FAR, A)
    z_pass(1, 1, A)
    z_pass(1, -1, B)
    choose(0, A)
    x_pass(NEAR, B)
    x_pass(FAR, B)
    z_pass(1, 1, B)
    z_pass(1, -1, A)
    choose(0, B)
    y_pass(1, 1, 0, A)
    y_pass(1, -1, 0, A)
    x_pass(OPPOSITE, A)
    x_pass(OPPOSITE, B)
    z_pass(2, 1, A)
    z_pass(2, -1, B)
    choose(1, A)
    y_pass(1, 1, 0, B)
    y_pass(1, -1, 0, B)
    choose(1, B)
    z_pass(2, 1, B)
    z_pass(2, -1, A)
    label_columns((0, 1, 7, 2))
    y_pass(2, 1, 0, A)
    y_pass(2, -1, 0, B)
    slope_quarter(0, 0)
    z_pass(3, 1, A)
    z_pass(3, -1, B)
    y_pass(1, 1, 1, A)
    y_pass(1, -1, 1, A)
    y_pass(1, 1, 1, B)
    y_pass(1, -1, 1, B)
    z_pass(3, 1, B)
    z_pass(3, -1, A)
    y_pass(2, 1, 1, A)
    y_pass(2, -1, 1, B)
    slope_quarter(0, 1)
    z_pass(4, 1, A)
    z_pass(4, -1, B)
    label_columns((6, 3, 5, 4))
    slope_quarter(1, 0)
    slope_quarter(1, 1)

    def grad_images(first, count):
        gi[first * rows:(first + count) * rows, :] = jnp.dot(
            slopes[first * rows:(first + count) * rows, :], tbuf[...], preferred_element_type=jnp.float32)

    def grad_texts(first, count):
        gt[first * rows:(first + count) * rows, :] = jnp.dot(
            slopes_t[first * rows:(first + count) * rows, :], ibuf[...], preferred_element_type=jnp.float32)

    def packed(out, value):
        tops = jnp.max(jnp.abs(value).reshape(half // SCALE_ROWS, SCALE_ROWS, width), axis=0)
        top = tops[:, 0:LANES]
        for t in range(1, tiles):
            top = jnp.maximum(top, tops[:, t * LANES:(t + 1) * LANES])
        exponent = jnp.ceil(jnp.log2(jnp.maximum(top, 1e-30)))
        inverse = jnp.concatenate([jnp.exp2(TOP - exponent)] * (half // SCALE_ROWS), axis=0)
        out[tiles * half:tiles * half + SCALE_ROWS, :] = exponent.astype(jnp.int16)
        for t in range(tiles):
            scaled = jnp.round(value[:, t * LANES:(t + 1) * LANES] * inverse)
            out[t * half:(t + 1) * half, :] = scaled.astype(jnp.int32).astype(jnp.int16)

    def unpacked(message):
        exponent = message[tiles * half:tiles * half + SCALE_ROWS, :].astype(jnp.int32).astype(jnp.float32)
        scale = jnp.concatenate([jnp.exp2(exponent - TOP)] * (half // SCALE_ROWS), axis=0)
        return jnp.concatenate(
            [message[t * half:(t + 1) * half, :].astype(jnp.int32).astype(jnp.float32) * scale for t in range(tiles)],
            axis=1)

    def ring(kind, n, out, inbox, up, down, partial):
        halfway = n // 2

        def slot(hop, way, chunk):
            return (0 if way > 0 else 1), 2 * (hop - 1) + chunk

        def get(hop, way, chunk):
            box = inbox.at[slot(hop, way, chunk)]
            arrived((kind, hop, way, chunk), box, up)
            return unpacked(box)

        def put(hop, way, chunk):
            value = partial(way * (halfway + 1 - hop), chunk)
            fresh = hop == 1 or (hop == 2 and chunk == (B if way > 0 else A))
            if not fresh:
                value = value + get(hop - 1, way, chunk)
            at = slot(hop, way, chunk)
            packed(out.at[at], value)
            send((kind, hop, way, chunk), out.at[at], inbox.at[at], up if way > 0 else down)

        def last(chunk):
            return partial(0, chunk) + get(halfway, 1, chunk) + get(halfway, -1, chunk)

        return put, last

    z_put, z_last = ring("gz", NZ, zq_out, zq_in, z_up, z_down,
                         lambda rel, chunk: gi[image_at(rel, chunk):image_at(rel, chunk) + half, :])
    y_puts, y_lasts = [], []
    for p in (0, 1):
        put, last = ring(("gy", p), NY, yq_out.at[p], yq_in.at[p], y_up, y_down,
                         lambda rel, chunk, p=p: gt[text_at(rel, p, chunk):text_at(rel, p, chunk) + half, :])
        y_puts.append(put)
        y_lasts.append(last)

    loss_stages = [(1, core, [(1, twin)]), (NX, x, x_others), (NY, y, y_others), (NZ, z, z_others)]

    def loss_send(stage):
        _, at, others = loss_stages[stage]
        loss_in[stage, at] = loss_acc[stage]
        for d, peer in others:
            send(("loss", stage, d), loss_acc.at[stage], loss_in.at[stage, at], peer)

    def loss_get(stage):
        _, at, others = loss_stages[stage]
        for d, peer in others:
            arrived(("loss", stage, d), loss_in.at[stage, at], peer)
        total = loss_in[stage, 0]
        for k in range(1, len(others) + 1):
            total = total + loss_in[stage, k]
        loss_acc[stage + 1] = total

    def y_finish(p, chunk):
        tsum[p, part(chunk)] = y_lasts[p](chunk)
        packed(sq_out.at[p, chunk], tsum[p, part(chunk)])
        send(("gs", p, chunk), sq_out.at[p, chunk], sq_in.at[p, chunk], twin)

    def twin_get(p, chunk):
        arrived(("gs", p, chunk), sq_in.at[p, chunk], twin)

    def weight(who, home):
        return jnp.full((1, LANES), jnp.where(partner_ref[who] == home, 1.0, 0.0), jnp.float32)

    twin_group, across = x_lo * 2 + (1 - core), (1 - x_lo) * 2 + core
    here_weights = weight(group, group), weight(twin_group, group)
    there_weights = weight(group, across), weight(twin_group, across)

    def x_partial(what, chunk):
        p, (own_weight, twin_weight) = {
            OWN: (0, here_weights), NEAR: (0, there_weights), FAR: (1, there_weights), OPPOSITE: (1, here_weights)}[what]
        own, other = tsum[p, part(chunk)], unpacked(sq_in.at[p, chunk])
        return jnp.concatenate(
            [own[:, t * LANES:(t + 1) * LANES] * own_weight + other[:, t * LANES:(t + 1) * LANES] * twin_weight
             for t in range(tiles)], axis=1)

    def x_get(what, chunk):
        arrived(("gx", what, chunk), xq_in.at[what, chunk], near)
        return unpacked(xq_in.at[what, chunk])

    def x_put(what, chunk):
        value = x_partial(what, chunk)
        if what == (FAR if chunk == A else NEAR):
            value = value + x_get(OPPOSITE, chunk)
        packed(xq_out.at[what, chunk], value)
        peer = {NEAR: near, FAR: far, OPPOSITE: near if chunk == A else far}[what]
        send(("gx", what, chunk), xq_out.at[what, chunk], xq_in.at[what, chunk], peer)

    def write(out, chunk, value):
        for t in range(tiles):
            out[0, part(chunk), t * LANES:(t + 1) * LANES] = temper * value[:, t * LANES:(t + 1) * LANES]

    loss_send(0)
    grad_texts(4, 4)
    y_puts[1](1, 1, A)
    y_puts[1](1, -1, B)
    y_puts[1](2, 1, B)
    y_puts[1](2, -1, A)
    grad_images(5, 3)
    z_put(1, 1, A)
    z_put(1, -1, B)
    z_put(2, 1, B)
    z_put(2, -1, A)
    loss_get(0)
    loss_send(1)
    grad_texts(0, 4)
    y_puts[0](1, 1, A)
    y_puts[0](1, -1, B)
    grad_images(0, 5)
    y_puts[1](2, 1, A)
    y_puts[1](2, -1, B)
    z_put(2, 1, A)
    z_put(2, -1, B)
    z_put(3, 1, B)
    z_put(3, -1, A)
    y_puts[0](2, 1, A)
    y_puts[0](2, -1, A)
    y_puts[0](2, 1, B)
    y_puts[0](2, -1, B)
    loss_get(1)
    loss_send(2)
    z_put(3, 1, A)
    z_put(3, -1, B)
    y_finish(1, A)
    y_finish(1, B)
    z_put(4, 1, B)
    z_put(4, -1, A)
    twin_get(1, A)
    x_put(OPPOSITE, A)
    twin_get(1, B)
    x_put(OPPOSITE, B)
    x_put(FAR, B)
    loss_get(2)
    loss_send(3)
    y_finish(0, A)
    z_put(4, 1, A)
    z_put(4, -1, B)
    twin_get(0, A)
    x_put(NEAR, A)
    x_put(FAR, A)
    y_finish(0, B)
    twin_get(0, B)
    x_put(NEAR, B)
    loss_get(3)
    loss_out[0] = jnp.sum(loss_acc[4]) / total_pairs
    for chunk in (A, B):
        write(img_out, chunk, z_last(chunk))
    for chunk in (A, B):
        write(txt_out, chunk, x_partial(OWN, chunk) + x_get(NEAR, chunk) + x_get(FAR, chunk))
    for copy in pending:
        copy.wait_send()


def shards(image_embeds, text_embeds, positives, partner, log_temp, bias):
    _, rows, width = image_embeds.shape
    half, tiles = rows // 2, width // LANES
    message = (tiles * half + SCALE_ROWS, LANES)
    n_i, n_t = NZ * rows, 2 * NY * rows
    cycle, groups = lax.axis_size("blk"), lax.axis_size("group")
    total_pairs = groups * rows * cycle * cycle
    vmem = pl.BlockSpec(memory_space=pltpu.VMEM)
    smem = pl.BlockSpec(memory_space=pltpu.SMEM)
    anywhere = pl.BlockSpec(memory_space=pl.ANY)
    f32, bf16, i16, i32 = jnp.float32, jnp.bfloat16, jnp.int16, jnp.int32
    copies = 112
    return pl.pallas_call(
        functools.partial(kernel, float(total_pairs)),
        out_shape=(jax.ShapeDtypeStruct((1, rows, width), f32), jax.ShapeDtypeStruct((1, rows, width), f32),
                   jax.ShapeDtypeStruct((1,), f32)),
        in_specs=[anywhere] * 6,
        out_specs=(vmem, vmem, smem),
        scratch_shapes=[
            pltpu.SMEM(partner.shape, i32),
            pltpu.SMEM((1,), f32),
            pltpu.SMEM((1,), f32),
            pltpu.VMEM((1, rows), i32),
            pltpu.VMEM((n_i, width), bf16),
            pltpu.VMEM((n_t, width), bf16),
            pltpu.VMEM((2, NX, rows, width), bf16),
            pltpu.VMEM((NZ, 8, LANES), i32),
            pltpu.VMEM((n_i, LANES), i32),
            pltpu.VMEM((n_i, n_t), bf16),
            pltpu.VMEM((n_t, n_i), bf16),
            pltpu.VMEM((n_i, width), f32),
            pltpu.VMEM((n_t, width), f32),
            pltpu.VMEM((2, rows, width), f32),
            pltpu.VMEM((5, 8, LANES), f32),
            pltpu.VMEM((4, NZ, 8, LANES), f32),
            pltpu.VMEM((2, NZ, *message), i16),
            pltpu.VMEM((2, NZ, *message), i16),
            pltpu.VMEM((2, 2, NY, *message), i16),
            pltpu.VMEM((2, 2, NY, *message), i16),
            pltpu.VMEM((2, 2, *message), i16),
            pltpu.VMEM((2, 2, *message), i16),
            pltpu.VMEM((NX, 2, *message), i16),
            pltpu.VMEM((NX, 2, *message), i16),
            pltpu.SemaphoreType.DMA((copies,)),
            pltpu.SemaphoreType.DMA((copies,)),
            pltpu.SemaphoreType.DMA((6,)),
        ],
        compiler_params=pltpu.CompilerParams(
            collective_id=0, has_side_effects=True, vmem_limit_bytes=48 * 1024 * 1024),
    )(partner, log_temp, bias, image_embeds, text_embeds, positives)


def solution(mesh):
    in_specs = (P("group", "blk", None), P("group", "blk", None), P("group", "blk"), P(), P(), P())
    out_specs = (P("group", "blk", None), P("group", "blk", None), P())
    return jax.shard_map(shards, mesh=mesh, in_specs=in_specs, out_specs=out_specs, check_vma=False)
```

time: 310 us -> 78.7 us (0.25)
  waiting for transfers between devices: 168 us -> 0 us
  blocking collectives: 98.8 us -> 0 us
  Pallas kernels: 0 us -> 71.4 us
  matrix products: 15.3 us -> 0 us
  between operations: 18.8 us -> 3.74 us
  local copies, waits for them, and re-layouts: 7.86 us -> 3.4 us
    all_gather x3 -> x0, waiting for transfers between devices: 84.5 us -> none  [the longest x1 60.9 us: shards(): lax.all_gather(images, 'blk', axis=0, tiled=True, axis_index_groups=acros...]
    reduce_scatter x2 -> x0, waiting for transfers between devices: 82.3 us -> none  [the longest x1 48.1 us: shards(): lax.psum_scatter(text_part, 'blk', scatter_dimension=0, tiled=True, axis_...]
    psum x1 -> x0, blocking collectives: 77.7 us -> none  [shards(): total = lax.psum(part, ('blk', 'group'))]
    pallas_call x0 -> x1, Pallas kernels: none -> 71.4 us  [shards(): pl.pallas_call(functools.partial(kernel, float(total_pairs)), out_shape=(...]
    dot_general x3 -> x0, matrix products: 15.3 us -> none  [the longest x1 5.85 us: pair_block(): jnp.dot(images, texts.T, preferred_element_type=jnp.float32)]
    all_gather x1 -> x0, blocking collectives: 10.8 us -> none  [shards(): every_text = lax.all_gather(own_texts, 'group', axis=0, tiled=True)]
    unnamed x1 -> x0, blocking collectives: 10.4 us -> none
  transfers between devices with their start and end apart: 5 -> 0, of which waited for: 4 -> 0; matrix products, arithmetic and copies ran while one was open for 3% -> 0% of each run, Pallas kernels for 0% -> 0%
where the time goes in v3:
time: 78.7 us; the launch traced here: 78.5 us
  Pallas kernels  71.4 us (91%)
  between operations  3.74 us (5%)
  local copies, waits for them, and re-layouts  3.4 us (4%)
    pallas_call x1, Pallas kernels, shards(): pl.pallas_call(functools.partial(kernel, float(total_pairs)), out_shape=(...  71.4 us
    unnamed x10, local copies, waits for them, and re-layouts  3.4 us

profile of v3, /device:TPU:1, one launch (start us, length us, event | category | flops | bytes accessed | tf_op | source)
XLA Modules:
  0.0 78.5 jit_solution(12409943974485216396)
XLA Ops:
  1.3 0.0 copy-start.2
  1.3 0.0 copy-start.3
  2.0 0.0 copy-done.2
  2.0 0.0 copy-done.3
  2.0 0.0 copy-start
  2.0 0.9 %copy-done = bf16[1,96,1152]{2,1,0:T(8,128)(2,1)S(1)} copy-done((bf16[1,96,1152]{2,1,0:T(8,128)(2,1)S(1)}, bf16[1,96,1152]{2,1,0:T(8,128)(2,1)}, u32[]{:S(2)}) %copy-start) | copy-done | bytes 221208
  2.9 0.0 copy-start.1
  2.9 0.9 %copy-done.1 = bf16[1,96,1152]{2,1,0:T(8,128)(2,1)S(1)} copy-done((bf16[1,96,1152]{2,1,0:T(8,128)(2,1)S(1)}, bf16[1,96,1152]{2,1,0:T(8,128)(2,1)}, u32[]{:S(2)}) %copy-start.1) | copy-done | bytes 221208
  3.9 71.4 %shard_map.85 = (f32[1,96,1152]{2,1,0:T(8,128)S(1)}, f32[1,96,1152]{2,1,0:T(8,128)S(1)}, f32[1]{0:T(128)}) custom-call(s32[4]{0:T(128)S(1)} %copy-done.2, f32[1]{0:T(128)S(6)} %copy.12.temp_in, f32[1]{0:T(128)S(6)} %copy.13.bias_in, bf16[1,96,1152]{2,1,0:T(8,128)(2,1)S(1)} %copy-done, bf16[1,96,1152]{2,1,0:T(8,128)(2,1)S(1)} %copy-done.1, s32[1,96]{1,0:T(1,128)S(1)} %copy-done.3), custom_call_target="tpu_custom_call" | custom-call | tf_op jit(solution)/shard_map/pallas_call | solution.py:434
  75.3 0.8 copy.14
  76.0 0.8 copy.15
Async XLA Ops:
  1.3 0.7 copy-start.2
  1.3 0.7 copy-start.3
  2.0 0.9 %copy-start = (bf16[1,96,1152]{2,1,0:T(8,128)(2,1)S(1)}, bf16[1,96,1152]{2,1,0:T(8,128)(2,1)}, u32[]{:S(2)}) copy-start(bf16[1,96,1152]{2,1,0:T(8,128)(2,1)} %img_in.1) | copy-start | bytes 663556
  2.9 0.9 %copy-start.1 = (bf16[1,96,1152]{2,1,0:T(8,128)(2,1)S(1)}, bf16[1,96,1152]{2,1,0:T(8,128)(2,1)}, u32[]{:S(2)}) copy-start(bf16[1,96,1152]{2,1,0:T(8,128)(2,1)} %txt_in.1) | copy-start | bytes 663556

commit v4 on v3

--- a/solution.py
+++ b/solution.py
@@ -9,6 +9,7 @@
 
 NZ, NX, NY = 8, 4, 4
 LANES = 128
+PIECES = 6
 SCALE_ROWS = 16
 TOP = 14.9657842846620869
 
@@ -19,7 +20,7 @@
            loss_acc, loss_in, zq_out, zq_in, yq_out, yq_in, sq_out, sq_in, xq_out, xq_in,
            send_sems, recv_sems, local_sems):
     rows, width = img_in.shape[1], img_in.shape[2]
-    half = rows // 2
+    half, piece = rows // 2, rows // PIECES
     tiles = width // LANES
     A, B = 0, 1
     OWN, NEAR, FAR, OPPOSITE = 0, 1, 2, 3
@@ -71,26 +72,29 @@
     def part(chunk):
         return pl.ds(chunk * half, half)
 
-    order = (0, 1, 7, 2, 6, 3, 5, 4)
+    order, text_order = (0, 1, 7, 2, 6, 3, 5, 4), (0, 1, 3, 2)
 
     def image_at(rel, chunk=0):
         return order.index(rel % NZ) * rows + chunk * half
 
     def text_at(rel, p, chunk=0):
-        return (p * NY + rel % NY) * rows + chunk * half
+        return (p * NY + text_order.index(rel % NY)) * rows + chunk * half
 
     def image_slot(rel, chunk):
         return ibuf.at[pl.ds(image_at(rel, chunk), half)]
 
-    def text_slot(rel, p, chunk):
-        return tbuf.at[pl.ds(text_at(rel, p, chunk), half)]
-
-    def x_slot(side, which, chunk):
-        return xbuf.at[side, which, part(chunk)]
+    def text_slot(rel, p, k):
+        return tbuf.at[pl.ds(text_at(rel, p) + k * piece, piece)]
+
+    def x_slot(side, which, k):
+        return xbuf.at[side, which, pl.ds(k * piece, piece)]
+
+    def low(k):
+        return k < PIECES // 2
 
     def z_send(hop, way, chunk):
-        send(("z", hop, way, chunk), image_slot(-way * (hop - 1), chunk), image_slot(-way * hop, chunk),
-             z_up if way > 0 else z_down)
+        source = img_in.at[0, part(chunk)] if hop == 1 else image_slot(-way * (hop - 1), chunk)
+        send(("z", hop, way, chunk), source, image_slot(-way * hop, chunk), z_up if way > 0 else z_down)
         if chunk == (A if way > 0 else B) and (way > 0 or hop < NZ // 2):
             send(("label", hop, way), labrow.at[(-way * (hop - 1)) % NZ], labrow.at[(-way * hop) % NZ],
                  z_up if way > 0 else z_down)
@@ -105,56 +109,66 @@
         if hop < NZ // 2 - 1 or (hop == NZ // 2 - 1 and chunk == (A if way > 0 else B)):
             z_send(hop + 1, way, chunk)
 
-    def x_send(what, chunk):
-        src, peer = {NEAR: (OWN, near), FAR: (OWN, far), OPPOSITE: (NEAR, far) if chunk == A else (FAR, near)}[what]
-        send(("x", what, chunk), x_slot(0, src, chunk), x_slot(0, what, chunk), peer)
-
-    def twin_send(what, chunk):
-        send(("twin", what, chunk), x_slot(0, what, chunk), x_slot(1, what, chunk), twin)
-
-    def x_pass(what, chunk):
-        arrived(("x", what, chunk), x_slot(0, what, chunk), near)
-        if what == (NEAR if chunk == A else FAR):
-            x_send(OPPOSITE, chunk)
-        twin_send(what, chunk)
-
-    def y_send(hop, way, p, chunk):
-        send(("y", hop, way, p, chunk), text_slot(-way * (hop - 1), p, chunk), text_slot(-way * hop, p, chunk),
+    def x_send(what, k):
+        src, peer = {NEAR: (OWN, near), FAR: (OWN, far), OPPOSITE: (NEAR, far) if low(k) else (FAR, near)}[what]
+        source = txt_in.at[0, pl.ds(k * piece, piece)] if src == OWN else x_slot(0, src, k)
+        send(("x", what, k), source, x_slot(0, what, k), peer)
+
+    def twin_send(what, k):
+        source = txt_in.at[0, pl.ds(k * piece, piece)] if what == OWN else x_slot(0, what, k)
+        send(("twin", what, k), source, x_slot(1, what, k), twin)
+
+    def x_pass(what, k):
+        arrived(("x", what, k), x_slot(0, what, k), near)
+        if what == (NEAR if low(k) else FAR):
+            x_send(OPPOSITE, k)
+        twin_send(what, k)
+
+    def y_send(hop, way, p, k):
+        send(("y", hop, way, p, k), text_slot(-way * (hop - 1), p, k), text_slot(-way * hop, p, k),
              y_up if way > 0 else y_down)
 
-    def y_pass(hop, way, p, chunk):
-        arrived(("y", hop, way, p, chunk), text_slot(-way * hop, p, chunk), y_up)
-        if hop == 1 and chunk == (A if way > 0 else B):
-            y_send(2, way, p, chunk)
-
-    def choose(p, chunk):
+    def y_pass(hop, way, p, k):
+        arrived(("y", hop, way, p, k), text_slot(-way * hop, p, k), y_up)
+        if hop == 1 and low(k) == (way > 0):
+            y_send(2, way, p, k)
+
+    def choose(p, k):
         target = partner_ref[group]
         same_side, same_core = target // 2 == x_lo, target % 2 == core
         here, there = (OWN, NEAR) if p == 0 else (OPPOSITE, FAR)
         for what in (here, there):
-            arrived(("twin", what, chunk), x_slot(1, what, chunk), twin)
-        here, there = (jnp.where(same_core, xbuf[0, what, part(chunk)], xbuf[1, what, part(chunk)])
+            arrived(("twin", what, k), x_slot(1, what, k), twin)
+        here, there = (jnp.where(same_core, xbuf[0, what, pl.ds(k * piece, piece)], xbuf[1, what, pl.ds(k * piece, piece)])
                        for what in (here, there))
-        tbuf[pl.ds(text_at(0, p, chunk), half), :] = jnp.where(same_side, here, there)
-        y_send(1, 1, p, chunk)
-        y_send(1, -1, p, chunk)
-
-    local[0].wait()
-    x_send(NEAR, A)
-    x_send(FAR, A)
-    local[1].wait()
+        tbuf[pl.ds(text_at(0, p) + k * piece, piece), :] = jnp.where(same_side, here, there)
+
+    x_send(NEAR, 0)
+    x_send(FAR, 3)
+    twin_send(OWN, 0)
     local[2].wait()
     labrow[0] = jnp.zeros((8, LANES), jnp.int32)
     labrow[0, 0:1, 0:rows] = lab_own[...]
     z_send(1, 1, A)
     z_send(1, -1, B)
-    twin_send(OWN, A)
-    twin_send(OWN, B)
-    x_send(NEAR, B)
-    x_send(FAR, B)
     z_send(1, 1, B)
     z_send(1, -1, A)
-    for copy in local[3:]:
+    x_send(NEAR, 1)
+    x_send(FAR, 4)
+    twin_send(OWN, 1)
+    x_send(NEAR, 2)
+    x_send(FAR, 5)
+    twin_send(OWN, 2)
+    x_send(NEAR, 3)
+    x_send(FAR, 0)
+    twin_send(OWN, 3)
+    x_send(NEAR, 4)
+    x_send(FAR, 1)
+    twin_send(OWN, 4)
+    x_send(NEAR, 5)
+    x_send(FAR, 2)
+    twin_send(OWN, 5)
+    for copy in local[:2] + local[3:]:
         copy.wait()
 
     temper = jnp.exp(jnp.full((1, LANES), temp_ref[0], jnp.float32))
@@ -167,79 +181,153 @@
             column = jnp.broadcast_to(labrow[rel, 0:1, :], (LANES, LANES)).T
             labcol[image_at(rel):image_at(rel) + rows, :] = column[:rows]
 
-    def slope_quarter(i_half, p):
-        left = p * NY * rows
-        wide = NY * rows
+    def slope_tiles(first, count, left, right):
+        wide = 2 * LANES
+        blocks = [(p, rel) for p in (0, 1) for rel in text_order]
+
+        def text_rows(at):
+            column = lax.broadcasted_iota(jnp.int32, (1, LANES), 1) + at
+            found = column
+            for b, (p, rel) in enumerate(blocks):
+                owner = (z * (NX // 2) + (x_hi + p) % 2) * NY + (y + rel) % NY
+                found = jnp.where(column >= b * rows, column + (owner - b) * rows, found)
+            return found
 
         def step(k, carry):
-            top = pl.multiple_of(i_half * (n_i // 2) + k * LANES, LANES)
-            dots = lax.dot_general(ibuf[pl.ds(top, LANES), :], tbuf[left:left + wide, :], (((1,), (1,)), ((), ())),
-                                   preferred_element_type=jnp.float32)
-            for at in range(0, wide, LANES):
-                logits = temper * dots[:, at:at + LANES] + offset
-                column = lax.broadcasted_iota(jnp.int32, (1, LANES), 1) + at
-                own = column + ((z * (NX // 2) + (x_hi + p) % 2) * NY + y) * rows
-                for b in range(1, NY):
-                    owner = (z * (NX // 2) + (x_hi + p) % 2) * NY + (y + b) % NY
-                    own = jnp.where(column >= b * rows, column + (owner - b) * rows, own)
-                hit = labcol[pl.ds(top, LANES), :] == own
-                margin = jnp.where(hit, -logits, logits)
-                small = jnp.exp(-jnp.abs(logits))
-                base = 1.0 + small
-                inverse = 1.0 / base
-                log_part = jnp.log(base) + (small - (base - 1.0)) * inverse
-                loss = jnp.maximum(margin, 0.0) + log_part
-                loss_acc[0] += jnp.sum(loss.reshape(LANES // 8, 8, LANES), axis=0)
-                slope = jnp.where(margin >= 0.0, 1.0, small) * inverse
-                slope = jnp.where(hit, -slope, slope).astype(jnp.bfloat16)
-                slopes[pl.ds(top, LANES), left + at:left + at + LANES] = slope
-                slopes_t[left + at:left + at + LANES, pl.ds(top, LANES)] = slope.T
+            top = pl.multiple_of(k * wide, wide)
+            for start in range(left, right, wide):
+                stop = min(start + wide, right)
+                dots = lax.dot_general(ibuf[pl.ds(top, wide), :], tbuf[start:stop, :], (((1,), (1,)), ((), ())),
+                                       preferred_element_type=jnp.float32)
+                for at in range(start, stop, LANES):
+                    logits = temper * dots[:, at - start:at - start + LANES] + offset
+                    hit = labcol[pl.ds(top, wide), :] == text_rows(at)
+                    margin = jnp.where(hit, -logits, logits)
+                    small = jnp.exp(-jnp.abs(logits))
+                    base = 1.0 + small
+                    inverse = 1.0 / base
+                    log_part = jnp.log(base) + (small - (base - 1.0)) * inverse
+                    loss = jnp.maximum(margin, 0.0) + log_part
+                    loss_acc[0] += jnp.sum(loss.reshape(wide // 8, 8, LANES), axis=0)
+                    slope = jnp.where(margin >= 0.0, 1.0, small) * inverse
+                    slope = jnp.where(hit, -slope, slope).astype(jnp.bfloat16)
+                    slopes[pl.ds(top, wide), at:at + LANES] = slope
+                    slopes_t[at:at + LANES, pl.ds(top, wide)] = slope.T
             return carry
 
-        lax.fori_loop(0, n_i // 2 // LANES, step, 0)
-
-    x_pass(NEAR, A)
-    x_pass(FAR, A)
+        lax.fori_loop(first, first + count, step, 0)
+
+    x_pass(NEAR, 0)
+    x_pass(FAR, 3)
+    x_pass(NEAR, 1)
+    x_pass(FAR, 4)
+    choose(0, 0)
+    y_send(1, 1, 0, 0)
+    y_send(1, -1, 0, 0)
+    x_pass(NEAR, 2)
+    x_pass(FAR, 5)
     z_pass(1, 1, A)
     z_pass(1, -1, B)
-    choose(0, A)
-    x_pass(NEAR, B)
-    x_pass(FAR, B)
+    choose(0, 1)
+    y_send(1, 1, 0, 1)
+    y_send(1, -1, 0, 1)
+    x_pass(NEAR, 3)
+    x_pass(FAR, 0)
+    choose(0, 2)
+    y_send(1, 1, 0, 2)
+    y_send(1, -1, 0, 2)
+    x_pass(NEAR, 4)
+    x_pass(FAR, 1)
+    choose(0, 3)
+    y_send(1, -1, 0, 3)
+    y_send(1, 1, 0, 3)
+    x_pass(NEAR, 5)
+    x_pass(FAR, 2)
     z_pass(1, 1, B)
     z_pass(1, -1, A)
-    choose(0, B)
-    y_pass(1, 1, 0, A)
-    y_pass(1, -1, 0, A)
-    x_pass(OPPOSITE, A)
-    x_pass(OPPOSITE, B)
+    y_pass(1, 1, 0, 0)
+    y_pass(1, -1, 0, 0)
+    choose(0, 4)
+    y_send(1, -1, 0, 4)
+    y_send(1, 1, 0, 4)
+    x_pass(OPPOSITE, 3)
+    x_pass(OPPOSITE, 0)
+    y_pass(1, 1, 0, 1)
+    y_pass(1, -1, 0, 1)
+    choose(0, 5)
+    y_send(1, -1, 0, 5)
+    y_send(1, 1, 0, 5)
+    x_pass(OPPOSITE, 4)
+    x_pass(OPPOSITE, 1)
+    y_pass(1, 1, 0, 2)
+    y_pass(1, -1, 0, 2)
+    choose(1, 3)
+    y_send(1, -1, 1, 3)
+    choose(1, 0)
+    y_send(1, 1, 1, 0)
+    x_pass(OPPOSITE, 5)
+    x_pass(OPPOSITE, 2)
     z_pass(2, 1, A)
     z_pass(2, -1, B)
-    choose(1, A)
-    y_pass(1, 1, 0, B)
-    y_pass(1, -1, 0, B)
-    choose(1, B)
+    y_pass(1, 1, 0, 3)
+    y_pass(1, -1, 0, 3)
+    choose(1, 4)
+    y_send(1, -1, 1, 4)
+    choose(1, 1)
+    y_send(1, 1, 1, 1)
+    y_pass(2, 1, 0, 0)
+    y_pass(1, -1, 0, 4)
+    choose(1, 5)
+    y_send(1, -1, 1, 5)
+    choose(1, 2)
+    y_send(1, 1, 1, 2)
+    y_pass(1, 1, 0, 4)
+    y_pass(1, -1, 0, 5)
+    y_send(1, 1, 1, 3)
+    y_send(1, -1, 1, 0)
+    y_send(1, 1, 1, 4)
+    y_send(1, -1, 1, 1)
+    y_send(1, 1, 1, 5)
+    y_send(1, -1, 1, 2)
     z_pass(2, 1, B)
     z_pass(2, -1, A)
     label_columns((0, 1, 7, 2))
-    y_pass(2, 1, 0, A)
-    y_pass(2, -1, 0, B)
-    slope_quarter(0, 0)
+    y_pass(2, 1, 0, 1)
+    y_pass(1, -1, 1, 3)
+    y_pass(1, 1, 0, 5)
+    y_pass(2, -1, 0, 3)
+    y_pass(2, 1, 0, 2)
+    y_pass(1, -1, 1, 4)
     z_pass(3, 1, A)
     z_pass(3, -1, B)
-    y_pass(1, 1, 1, A)
-    y_pass(1, -1, 1, A)
-    y_pass(1, 1, 1, B)
-    y_pass(1, -1, 1, B)
+    y_pass(1, 1, 1, 0)
+    y_pass(2, -1, 0, 4)
+    y_pass(1, 1, 1, 1)
+    y_pass(1, -1, 1, 5)
+    y_pass(1, 1, 1, 2)
+    y_pass(2, -1, 0, 5)
     z_pass(3, 1, B)
     z_pass(3, -1, A)
-    y_pass(2, 1, 1, A)
-    y_pass(2, -1, 1, B)
-    slope_quarter(0, 1)
+    label_columns((6, 3, 5))
+    slope_tiles(0, 2, 0, 3 * LANES)
+    y_pass(1, 1, 1, 3)
+    y_pass(1, -1, 1, 0)
+    y_pass(1, 1, 1, 4)
+    y_pass(1, -1, 1, 1)
+    y_pass(1, 1, 1, 5)
+    y_pass(1, -1, 1, 2)
     z_pass(4, 1, A)
     z_pass(4, -1, B)
-    label_columns((6, 3, 5, 4))
-    slope_quarter(1, 0)
-    slope_quarter(1, 1)
+    label_columns((4,))
+    slope_tiles(2, 1, 0, 3 * LANES)
+    slope_tiles(0, 3, 3 * LANES, 5 * LANES)
+    y_pass(2, 1, 1, 0)
+    y_pass(2, -1, 1, 3)
+    y_pass(2, 1, 1, 1)
+    y_pass(2, -1, 1, 4)
+    y_pass(2, 1, 1, 2)
+    y_pass(2, -1, 1, 5)
+    slope_tiles(0, 3, 5 * LANES, 6 * LANES)
 
     def grad_images(first, count):
         gi[first * rows:(first + count) * rows, :] = jnp.dot(
@@ -302,16 +390,16 @@
         y_puts.append(put)
         y_lasts.append(last)
 
-    loss_stages = [(1, core, [(1, twin)]), (NX, x, x_others), (NY, y, y_others), (NZ, z, z_others)]
+    loss_stages = [(z, z_others), (x, x_others), (core, [(1, twin)]), (y, y_others)]
 
     def loss_send(stage):
-        _, at, others = loss_stages[stage]
+        at, others = loss_stages[stage]
         loss_in[stage, at] = loss_acc[stage]
         for d, peer in others:
             send(("loss", stage, d), loss_acc.at[stage], loss_in.at[stage, at], peer)
 
     def loss_get(stage):
-        _, at, others = loss_stages[stage]
+        at, others = loss_stages[stage]
         for d, peer in others:
             arrived(("loss", stage, d), loss_in.at[stage, at], peer)
         total = loss_in[stage, 0]
@@ -355,42 +443,45 @@
         send(("gx", what, chunk), xq_out.at[what, chunk], xq_in.at[what, chunk], peer)
 
     def write(out, chunk, value):
-        for t in range(tiles):
-            out[0, part(chunk), t * LANES:(t + 1) * LANES] = temper * value[:, t * LANES:(t + 1) * LANES]
+        out[0, part(chunk), :] = value
 
     loss_send(0)
-    grad_texts(4, 4)
+    grad_texts(7, 1)
     y_puts[1](1, 1, A)
     y_puts[1](1, -1, B)
-    y_puts[1](2, 1, B)
-    y_puts[1](2, -1, A)
+    grad_texts(3, 1)
+    y_puts[0](1, 1, A)
+    y_puts[0](1, -1, B)
     grad_images(5, 3)
     z_put(1, 1, A)
     z_put(1, -1, B)
     z_put(2, 1, B)
     z_put(2, -1, A)
+    grad_texts(4, 3)
+    y_puts[1](2, 1, B)
+    y_puts[1](2, -1, A)
+    grad_texts(0, 3)
+    grad_images(0, 5)
     loss_get(0)
     loss_send(1)
-    grad_texts(0, 4)
-    y_puts[0](1, 1, A)
-    y_puts[0](1, -1, B)
-    grad_images(0, 5)
     y_puts[1](2, 1, A)
     y_puts[1](2, -1, B)
     z_put(2, 1, A)
     z_put(2, -1, B)
+    y_puts[0](2, 1, A)
+    y_puts[0](2, -1, A)
+    y_puts[0](2, -1, B)
+    y_puts[0](2, 1, B)
     z_put(3, 1, B)
     z_put(3, -1, A)
-    y_puts[0](2, 1, A)
-    y_puts[0](2, -1, A)
-    y_puts[0](2, 1, B)
-    y_puts[0](2, -1, B)
     loss_get(1)
     loss_send(2)
     z_put(3, 1, A)
     z_put(3, -1, B)
     y_finish(1, A)
     y_finish(1, B)
+    loss_get(2)
+    loss_send(3)
     z_put(4, 1, B)
     z_put(4, -1, A)
     twin_get(1, A)
@@ -398,15 +489,13 @@
     twin_get(1, B)
     x_put(OPPOSITE, B)
     x_put(FAR, B)
-    loss_get(2)
-    loss_send(3)
     y_finish(0, A)
     z_put(4, 1, A)
     z_put(4, -1, B)
     twin_get(0, A)
     x_put(NEAR, A)
+    y_finish(0, B)
     x_put(FAR, A)
-    y_finish(0, B)
     twin_get(0, B)
     x_put(NEAR, B)
     loss_get(3)
@@ -428,14 +517,15 @@
     total_pairs = groups * rows * cycle * cycle
     vmem = pl.BlockSpec(memory_space=pltpu.VMEM)
     smem = pl.BlockSpec(memory_space=pltpu.SMEM)
-    anywhere = pl.BlockSpec(memory_space=pl.ANY)
+    hbm = pl.BlockSpec(memory_space=pltpu.HBM)
+    in_hbm = functools.partial(pltpu.with_memory_space_constraint, memory_space=pltpu.HBM)
     f32, bf16, i16, i32 = jnp.float32, jnp.bfloat16, jnp.int16, jnp.int32
-    copies = 112
-    return pl.pallas_call(
+    copies = 176
+    images, texts, loss = pl.pallas_call(
         functools.partial(kernel, float(total_pairs)),
         out_shape=(jax.ShapeDtypeStruct((1, rows, width), f32), jax.ShapeDtypeStruct((1, rows, width), f32),
                    jax.ShapeDtypeStruct((1,), f32)),
-        in_specs=[anywhere] * 6,
+        in_specs=[hbm] * 6,
         out_specs=(vmem, vmem, smem),
         scratch_shapes=[
             pltpu.SMEM(partner.shape, i32),
@@ -468,7 +558,9 @@
         ],
         compiler_params=pltpu.CompilerParams(
             collective_id=0, has_side_effects=True, vmem_limit_bytes=48 * 1024 * 1024),
-    )(partner, log_temp, bias, image_embeds, text_embeds, positives)
+    )(in_hbm(partner), log_temp, bias, in_hbm(image_embeds), in_hbm(text_embeds), in_hbm(positives))
+    temper = jnp.exp(log_temp[0])
+    return temper * images, temper * texts, loss
 
 
 def solution(mesh):

time: 78.7 us -> 68.7 us (0.87)
  Pallas kernels: 71.4 us -> 63.9 us
  local copies, waits for them, and re-layouts: 3.4 us -> 0 us
  other arithmetic: 0 us -> 0.97 us
    pallas_call x1, Pallas kernels: 71.4 us -> 63.9 us  [shards(): pl.pallas_call(functools.partial(kernel, float(total_pairs)), out_shape=(...]
    unnamed x10 -> x0, local copies, waits for them, and re-layouts: 3.4 us -> none
    mul x0 -> x1, other arithmetic: none -> 0.97 us  [shards(): return (temper * images, temper * texts, loss)]
where the time goes in v4:
time: 68.7 us; the launch traced here: 68.6 us
  Pallas kernels  63.9 us (93%)
  between operations  3.74 us (5%)
  other arithmetic  0.97 us (1%)
    pallas_call x1, Pallas kernels, shards(): pl.pallas_call(functools.partial(kernel, float(total_pairs)), out_shape=(...  63.9 us

profile of v4, /device:TPU:1, one launch (start us, length us, event | category | flops | bytes accessed | tf_op | source)
XLA Modules:
  0.0 68.6 jit_solution(10074041532403024226)
XLA Ops:
  2.0 63.9 %shard_map.85 = (f32[1,96,1152]{2,1,0:T(8,128)S(1)}, f32[1,96,1152]{2,1,0:T(8,128)S(1)}, f32[1]{0:T(128)}) custom-call(s32[4]{0:T(128)} %partner_in.1, f32[1]{0:T(128)S(6)} %copy.10.temp_in, f32[1]{0:T(128)S(6)} %copy.11.bias_in, bf16[1,96,1152]{2,1,0:T(8,128)(2,1)} %img_in.1, bf16[1,96,1152]{2,1,0:T(8,128)(2,1)} %txt_in.1, s32[1,96]{1,0:T(1,128)} %lab_in.1), custom_call_target="tpu_custom_call" | custom-call | tf_op jit(solution)/shard_map/pallas_call | solution.py:524
  65.9 1.0 %broadcast_multiply_fusion = (f32[1,96,1152]{2,1,0:T(8,128)}, f32[1,96,1152]{2,1,0:T(8,128)}) fusion(f32[1,96,1152]{2,1,0:T(8,128)S(1)} %get-tuple-element.7, f32[]{:T(128)} %bitcast, f32[1,96,1152]{2,1,0:T(8,128)S(1)} %get-tuple-element.6), kind=kLoop, calls=%fused_computation | loop fusion | flops 221184 | bytes 1769476 | tf_op jit(solution)/shard_map/mul | solution.py:563

commit v5 on v4

--- a/solution.py
+++ b/solution.py
@@ -95,9 +95,12 @@
     def z_send(hop, way, chunk):
         source = img_in.at[0, part(chunk)] if hop == 1 else image_slot(-way * (hop - 1), chunk)
         send(("z", hop, way, chunk), source, image_slot(-way * hop, chunk), z_up if way > 0 else z_down)
-        if chunk == (A if way > 0 else B) and (way > 0 or hop < NZ // 2):
-            send(("label", hop, way), labrow.at[(-way * (hop - 1)) % NZ], labrow.at[(-way * hop) % NZ],
-                 z_up if way > 0 else z_down)
+        if hop > 1 and chunk == (A if way > 0 else B) and (way > 0 or hop < NZ // 2):
+            label_send(hop, way)
+
+    def label_send(hop, way):
+        send(("label", hop, way), labrow.at[(-way * (hop - 1)) % NZ], labrow.at[(-way * hop) % NZ],
+             z_up if way > 0 else z_down)
 
     def z_arrived(hop, way, chunk):
         arrived(("z", hop, way, chunk), image_slot(-way * hop, chunk), z_up)
@@ -146,9 +149,6 @@
     x_send(NEAR, 0)
     x_send(FAR, 3)
     twin_send(OWN, 0)
-    local[2].wait()
-    labrow[0] = jnp.zeros((8, LANES), jnp.int32)
-    labrow[0, 0:1, 0:rows] = lab_own[...]
     z_send(1, 1, A)
     z_send(1, -1, B)
     z_send(1, 1, B)
@@ -168,6 +168,11 @@
     x_send(NEAR, 5)
     x_send(FAR, 2)
     twin_send(OWN, 5)
+    local[2].wait()
+    labrow[0] = jnp.zeros((8, LANES), jnp.int32)
+    labrow[0, 0:1, 0:rows] = lab_own[...]
+    label_send(1, 1)
+    label_send(1, -1)
     for copy in local[:2] + local[3:]:
         copy.wait()
 
@@ -216,6 +221,122 @@
             return carry
 
         lax.fori_loop(first, first + count, step, 0)
+
+    def grad_images(first, count):
+        gi[first * rows:(first + count) * rows, :] = jnp.dot(
+            slopes[first * rows:(first + count) * rows, :], tbuf[...], preferred_element_type=jnp.float32)
+
+    def grad_texts(first, count):
+        gt[first * rows:(first + count) * rows, :] = jnp.dot(
+            slopes_t[first * rows:(first + count) * rows, :], ibuf[...], preferred_element_type=jnp.float32)
+
+    def packed(out, value):
+        tops = jnp.max(jnp.abs(value).reshape(half // SCALE_ROWS, SCALE_ROWS, width), axis=0)
+        top = tops[:, 0:LANES]
+        for t in range(1, tiles):
+            top = jnp.maximum(top, tops[:, t * LANES:(t + 1) * LANES])
+        exponent = jnp.ceil(jnp.log2(jnp.maximum(top, 1e-30)))
+        inverse = jnp.concatenate([jnp.exp2(TOP - exponent)] * (half // SCALE_ROWS), axis=0)
+        out[tiles * half:tiles * half + SCALE_ROWS, :] = exponent.astype(jnp.int16)
+        for t in range(tiles):
+            scaled = jnp.round(value[:, t * LANES:(t + 1) * LANES] * inverse)
+            out[t * half:(t + 1) * half, :] = scaled.astype(jnp.int32).astype(jnp.int16)
+
+    def unpacked(message):
+        exponent = message[tiles * half:tiles * half + SCALE_ROWS, :].astype(jnp.int32).astype(jnp.float32)
+        scale = jnp.concatenate([jnp.exp2(exponent - TOP)] * (half // SCALE_ROWS), axis=0)
+        return jnp.concatenate(
+            [message[t * half:(t + 1) * half, :].astype(jnp.int32).astype(jnp.float32) * scale for t in range(tiles)],
+            axis=1)
+
+    def ring(kind, n, out, inbox, up, down, partial):
+        halfway = n // 2
+
+        def slot(hop, way, chunk):
+            return (0 if way > 0 else 1), 2 * (hop - 1) + chunk
+
+        def get(hop, way, chunk):
+            box = inbox.at[slot(hop, way, chunk)]
+            arrived((kind, hop, way, chunk), box, up)
+            return unpacked(box)
+
+        def put(hop, way, chunk):
+            value = partial(way * (halfway + 1 - hop), chunk)
+            fresh = hop == 1 or (hop == 2 and chunk == (B if way > 0 else A))
+            if not fresh:
+                value = value + get(hop - 1, way, chunk)
+            at = slot(hop, way, chunk)
+            packed(out.at[at], value)
+            send((kind, hop, way, chunk), out.at[at], inbox.at[at], up if way > 0 else down)
+
+        def last(chunk):
+            return partial(0, chunk) + get(halfway, 1, chunk) + get(halfway, -1, chunk)
+
+        return put, last
+
+    z_put, z_last = ring("gz", NZ, zq_out, zq_in, z_up, z_down,
+                         lambda rel, chunk: gi[image_at(rel, chunk):image_at(rel, chunk) + half, :])
+    y_puts, y_lasts = [], []
+    for p in (0, 1):
+        put, last = ring(("gy", p), NY, yq_out.at[p], yq_in.at[p], y_up, y_down,
+                         lambda rel, chunk, p=p: gt[text_at(rel, p, chunk):text_at(rel, p, chunk) + half, :])
+        y_puts.append(put)
+        y_lasts.append(last)
+
+    loss_stages = [(z, z_others), (x, x_others), (core, [(1, twin)]), (y, y_others)]
+
+    def loss_send(stage):
+        at, others = loss_stages[stage]
+        loss_in[stage, at] = loss_acc[stage]
+        for d, peer in others:
+            send(("loss", stage, d), loss_acc.at[stage], loss_in.at[stage, at], peer)
+
+    def loss_get(stage):
+        at, others = loss_stages[stage]
+        for d, peer in others:
+            arrived(("loss", stage, d), loss_in.at[stage, at], peer)
+        total = loss_in[stage, 0]
+        for k in range(1, len(others) + 1):
+            total = total + loss_in[stage, k]
+        loss_acc[stage + 1] = total
+
+    def y_finish(p, chunk):
+        tsum[p, part(chunk)] = y_lasts[p](chunk)
+        packed(sq_out.at[p, chunk], tsum[p, part(chunk)])
+        send(("gs", p, chunk), sq_out.at[p, chunk], sq_in.at[p, chunk], twin)
+
+    def twin_get(p, chunk):
+        arrived(("gs", p, chunk), sq_in.at[p, chunk], twin)
+
+    def weight(who, home):
+        return jnp.full((1, LANES), jnp.where(partner_ref[who] == home, 1.0, 0.0), jnp.float32)
+
+    twin_group, across = x_lo * 2 + (1 - core), (1 - x_lo) * 2 + core
+    here_weights = weight(group, group), weight(twin_group, group)
+    there_weights = weight(group, across), weight(twin_group, across)
+
+    def x_partial(what, chunk):
+        p, (own_weight, twin_weight) = {
+            OWN: (0, here_weights), NEAR: (0, there_weights), FAR: (1, there_weights), OPPOSITE: (1, here_weights)}[what]
+        own, other = tsum[p, part(chunk)], unpacked(sq_in.at[p, chunk])
+        return jnp.concatenate(
+            [own[:, t * LANES:(t + 1) * LANES] * own_weight + other[:, t * LANES:(t + 1) * LANES] * twin_weight
+             for t in range(tiles)], axis=1)
+
+    def x_get(what, chunk):
+        arrived(("gx", what, chunk), xq_in.at[what, chunk], near)
+        return unpacked(xq_in.at[what, chunk])
+
+    def x_put(what, chunk):
+        value = x_partial(what, chunk)
+        if what == (FAR if chunk == A else NEAR):
+            value = value + x_get(OPPOSITE, chunk)
+        packed(xq_out.at[what, chunk], value)
+        peer = {NEAR: near, FAR: far, OPPOSITE: near if chunk == A else far}[what]
+        send(("gx", what, chunk), xq_out.at[what, chunk], xq_in.at[what, chunk], peer)
+
+    def write(out, chunk, value):
+        out[0, part(chunk), :] = value
 
     x_pass(NEAR, 0)
     x_pass(FAR, 3)
@@ -316,11 +437,15 @@
     y_pass(1, -1, 1, 1)
     y_pass(1, 1, 1, 5)
     y_pass(1, -1, 1, 2)
+    slope_tiles(0, 2, 3 * LANES, 5 * LANES)
     z_pass(4, 1, A)
     z_pass(4, -1, B)
     label_columns((4,))
     slope_tiles(2, 1, 0, 3 * LANES)
-    slope_tiles(0, 3, 3 * LANES, 5 * LANES)
+    grad_texts(0, 4)
+    y_puts[0](1, 1, A)
+    y_puts[0](1, -1, B)
+    slope_tiles(2, 1, 3 * LANES, 5 * LANES)
     y_pass(2, 1, 1, 0)
     y_pass(2, -1, 1, 3)
     y_pass(2, 1, 1, 1)
@@ -329,129 +454,10 @@
     y_pass(2, -1, 1, 5)
     slope_tiles(0, 3, 5 * LANES, 6 * LANES)
 
-    def grad_images(first, count):
-        gi[first * rows:(first + count) * rows, :] = jnp.dot(
-            slopes[first * rows:(first + count) * rows, :], tbuf[...], preferred_element_type=jnp.float32)
-
-    def grad_texts(first, count):
-        gt[first * rows:(first + count) * rows, :] = jnp.dot(
-            slopes_t[first * rows:(first + count) * rows, :], ibuf[...], preferred_element_type=jnp.float32)
-
-    def packed(out, value):
-        tops = jnp.max(jnp.abs(value).reshape(half // SCALE_ROWS, SCALE_ROWS, width), axis=0)
-        top = tops[:, 0:LANES]
-        for t in range(1, tiles):
-            top = jnp.maximum(top, tops[:, t * LANES:(t + 1) * LANES])
-        exponent = jnp.ceil(jnp.log2(jnp.maximum(top, 1e-30)))
-        inverse = jnp.concatenate([jnp.exp2(TOP - exponent)] * (half // SCALE_ROWS), axis=0)
-        out[tiles * half:tiles * half + SCALE_ROWS, :] = exponent.astype(jnp.int16)
-        for t in range(tiles):
-            scaled = jnp.round(value[:, t * LANES:(t + 1) * LANES] * inverse)
-            out[t * half:(t + 1) * half, :] = scaled.astype(jnp.int32).astype(jnp.int16)
-
-    def unpacked(message):
-        exponent = message[tiles * half:tiles * half + SCALE_ROWS, :].astype(jnp.int32).astype(jnp.float32)
-        scale = jnp.concatenate([jnp.exp2(exponent - TOP)] * (half // SCALE_ROWS), axis=0)
-        return jnp.concatenate(
-            [message[t * half:(t + 1) * half, :].astype(jnp.int32).astype(jnp.float32) * scale for t in range(tiles)],
-            axis=1)
-
-    def ring(kind, n, out, inbox, up, down, partial):
-        halfway = n // 2
-
-        def slot(hop, way, chunk):
-            return (0 if way > 0 else 1), 2 * (hop - 1) + chunk
-
-        def get(hop, way, chunk):
-            box = inbox.at[slot(hop, way, chunk)]
-            arrived((kind, hop, way, chunk), box, up)
-            return unpacked(box)
-
-        def put(hop, way, chunk):
-            value = partial(way * (halfway + 1 - hop), chunk)
-            fresh = hop == 1 or (hop == 2 and chunk == (B if way > 0 else A))
-            if not fresh:
-                value = value + get(hop - 1, way, chunk)
-            at = slot(hop, way, chunk)
-            packed(out.at[at], value)
-            send((kind, hop, way, chunk), out.at[at], inbox.at[at], up if way > 0 else down)
-
-        def last(chunk):
-            return partial(0, chunk) + get(halfway, 1, chunk) + get(halfway, -1, chunk)
-
-        return put, last
-
-    z_put, z_last = ring("gz", NZ, zq_out, zq_in, z_up, z_down,
-                         lambda rel, chunk: gi[image_at(rel, chunk):image_at(rel, chunk) + half, :])
-    y_puts, y_lasts = [], []
-    for p in (0, 1):
-        put, last = ring(("gy", p), NY, yq_out.at[p], yq_in.at[p], y_up, y_down,
-                         lambda rel, chunk, p=p: gt[text_at(rel, p, chunk):text_at(rel, p, chunk) + half, :])
-        y_puts.append(put)
-        y_lasts.append(last)
-
-    loss_stages = [(z, z_others), (x, x_others), (core, [(1, twin)]), (y, y_others)]
-
-    def loss_send(stage):
-        at, others = loss_stages[stage]
-        loss_in[stage, at] = loss_acc[stage]
-        for d, peer in others:
-            send(("loss", stage, d), loss_acc.at[stage], loss_in.at[stage, at], peer)
-
-    def loss_get(stage):
-        at, others = loss_stages[stage]
-        for d, peer in others:
-            arrived(("loss", stage, d), loss_in.at[stage, at], peer)
-        total = loss_in[stage, 0]
-        for k in range(1, len(others) + 1):
-            total = total + loss_in[stage, k]
-        loss_acc[stage + 1] = total
-
-    def y_finish(p, chunk):
-        tsum[p, part(chunk)] = y_lasts[p](chunk)
-        packed(sq_out.at[p, chunk], tsum[p, part(chunk)])
-        send(("gs", p, chunk), sq_out.at[p, chunk], sq_in.at[p, chunk], twin)
-
-    def twin_get(p, chunk):
-        arrived(("gs", p, chunk), sq_in.at[p, chunk], twin)
-
-    def weight(who, home):
-        return jnp.full((1, LANES), jnp.where(partner_ref[who] == home, 1.0, 0.0), jnp.float32)
-
-    twin_group, across = x_lo * 2 + (1 - core), (1 - x_lo) * 2 + core
-    here_weights = weight(group, group), weight(twin_group, group)
-    there_weights = weight(group, across), weight(twin_group, across)
-
-    def x_partial(what, chunk):
-        p, (own_weight, twin_weight) = {
-            OWN: (0, here_weights), NEAR: (0, there_weights), FAR: (1, there_weights), OPPOSITE: (1, here_weights)}[what]
-        own, other = tsum[p, part(chunk)], unpacked(sq_in.at[p, chunk])
-        return jnp.concatenate(
-            [own[:, t * LANES:(t + 1) * LANES] * own_weight + other[:, t * LANES:(t + 1) * LANES] * twin_weight
-             for t in range(tiles)], axis=1)
-
-    def x_get(what, chunk):
-        arrived(("gx", what, chunk), xq_in.at[what, chunk], near)
-        return unpacked(xq_in.at[what, chunk])
-
-    def x_put(what, chunk):
-        value = x_partial(what, chunk)
-        if what == (FAR if chunk == A else NEAR):
-            value = value + x_get(OPPOSITE, chunk)
-        packed(xq_out.at[what, chunk], value)
-        peer = {NEAR: near, FAR: far, OPPOSITE: near if chunk == A else far}[what]
-        send(("gx", what, chunk), xq_out.at[what, chunk], xq_in.at[what, chunk], peer)
-
-    def write(out, chunk, value):
-        out[0, part(chunk), :] = value
-
     loss_send(0)
     grad_texts(7, 1)
     y_puts[1](1, 1, A)
     y_puts[1](1, -1, B)
-    grad_texts(3, 1)
-    y_puts[0](1, 1, A)
-    y_puts[0](1, -1, B)
     grad_images(5, 3)
     z_put(1, 1, A)
     z_put(1, -1, B)
@@ -460,7 +466,6 @@
     grad_texts(4, 3)
     y_puts[1](2, 1, B)
     y_puts[1](2, -1, A)
-    grad_texts(0, 3)
     grad_images(0, 5)
     loss_get(0)
     loss_send(1)

time: 68.7 us -> 69.6 us (1.013); the launches traced: 68.6 us -> 68.8 us
  no operation moved by 1% of the time
where the time goes in v5:
time: 69.6 us; the launch traced here: 68.8 us
  Pallas kernels  64.1 us (92%)
  between operations  3.74 us (5%)
  other arithmetic  0.97 us (1%)
    pallas_call x1, Pallas kernels, shards(): pl.pallas_call(functools.partial(kernel, float(total_pairs)), out_shape=(...  64.1 us

profile of v5, /device:TPU:1, one launch (start us, length us, event | category | flops | bytes accessed | tf_op | source)
XLA Modules:
  0.0 68.8 jit_solution(4423256133997962559)
XLA Ops:
  2.0 64.1 %shard_map.85 = (f32[1,96,1152]{2,1,0:T(8,128)S(1)}, f32[1,96,1152]{2,1,0:T(8,128)S(1)}, f32[1]{0:T(128)}) custom-call(s32[4]{0:T(128)} %partner_in.1, f32[1]{0:T(128)S(6)} %copy.10.temp_in, f32[1]{0:T(128)S(6)} %copy.11.bias_in, bf16[1,96,1152]{2,1,0:T(8,128)(2,1)} %img_in.1, bf16[1,96,1152]{2,1,0:T(8,128)(2,1)} %txt_in.1, s32[1,96]{1,0:T(1,128)} %lab_in.1), custom_call_target="tpu_custom_call" | custom-call | tf_op jit(solution)/shard_map/pallas_call | solution.py:529
  66.1 1.0 %broadcast_multiply_fusion = (f32[1,96,1152]{2,1,0:T(8,128)}, f32[1,96,1152]{2,1,0:T(8,128)}) fusion(f32[1,96,1152]{2,1,0:T(8,128)S(1)} %get-tuple-element.7, f32[]{:T(128)} %bitcast, f32[1,96,1152]{2,1,0:T(8,128)S(1)} %get-tuple-element.6), kind=kLoop, calls=%fused_computation | loop fusion | flops 221184 | bytes 1769476 | tf_op jit(solution)/shard_map/mul | solution.py:568

commit v6 on v5

--- a/solution.py
+++ b/solution.py
@@ -95,22 +95,20 @@
     def z_send(hop, way, chunk):
         source = img_in.at[0, part(chunk)] if hop == 1 else image_slot(-way * (hop - 1), chunk)
         send(("z", hop, way, chunk), source, image_slot(-way * hop, chunk), z_up if way > 0 else z_down)
-        if hop > 1 and chunk == (A if way > 0 else B) and (way > 0 or hop < NZ // 2):
-            label_send(hop, way)
 
     def label_send(hop, way):
         send(("label", hop, way), labrow.at[(-way * (hop - 1)) % NZ], labrow.at[(-way * hop) % NZ],
              z_up if way > 0 else z_down)
 
-    def z_arrived(hop, way, chunk):
+    def z_pass(hop, way, chunk):
+        first = chunk == (A if way > 0 else B)
         arrived(("z", hop, way, chunk), image_slot(-way * hop, chunk), z_up)
-        if chunk == (A if way > 0 else B) and (way > 0 or hop < NZ // 2):
+        if hop < NZ // 2 - 1 or (hop == NZ // 2 - 1 and first):
+            z_send(hop + 1, way, chunk)
+        if not first or (hop == NZ // 2 and way > 0):
             arrived(("label", hop, way), labrow.at[(-way * hop) % NZ], z_up)
-
-    def z_pass(hop, way, chunk):
-        z_arrived(hop, way, chunk)
-        if hop < NZ // 2 - 1 or (hop == NZ // 2 - 1 and chunk == (A if way > 0 else B)):
-            z_send(hop + 1, way, chunk)
+            if hop < NZ // 2 - 1 or (hop == NZ // 2 - 1 and way > 0):
+                label_send(hop + 1, way)
 
     def x_send(what, k):
         src, peer = {NEAR: (OWN, near), FAR: (OWN, far), OPPOSITE: (NEAR, far) if low(k) else (FAR, near)}[what]

time: 69.6 us -> 68.3 us (0.981)
  Pallas kernels: 64.1 us -> 62.8 us
    pallas_call x1, Pallas kernels: 64.1 us -> 62.8 us  [shards(): pl.pallas_call(functools.partial(kernel, float(total_pairs)), out_shape=(...]
where the time goes in v6:
time: 68.3 us; the launch traced here: 67.5 us
  Pallas kernels  62.8 us (92%)
  between operations  3.74 us (5%)
  other arithmetic  0.97 us (1%)
    pallas_call x1, Pallas kernels, shards(): pl.pallas_call(functools.partial(kernel, float(total_pairs)), out_shape=(...  62.8 us

profile of v6, /device:TPU:1, one launch (start us, length us, event | category | flops | bytes accessed | tf_op | source)
XLA Modules:
  0.0 67.5 jit_solution(7832663950928931122)
XLA Ops:
  2.0 62.8 %shard_map.85 = (f32[1,96,1152]{2,1,0:T(8,128)S(1)}, f32[1,96,1152]{2,1,0:T(8,128)S(1)}, f32[1]{0:T(128)}) custom-call(s32[4]{0:T(128)} %partner_in.1, f32[1]{0:T(128)S(6)} %copy.10.temp_in, f32[1]{0:T(128)S(6)} %copy.11.bias_in, bf16[1,96,1152]{2,1,0:T(8,128)(2,1)} %img_in.1, bf16[1,96,1152]{2,1,0:T(8,128)(2,1)} %txt_in.1, s32[1,96]{1,0:T(1,128)} %lab_in.1), custom_call_target="tpu_custom_call" | custom-call | tf_op jit(solution)/shard_map/pallas_call | solution.py:527
  64.7 1.0 %broadcast_multiply_fusion = (f32[1,96,1152]{2,1,0:T(8,128)}, f32[1,96,1152]{2,1,0:T(8,128)}) fusion(f32[1,96,1152]{2,1,0:T(8,128)S(1)} %get-tuple-element.7, f32[]{:T(128)} %bitcast, f32[1,96,1152]{2,1,0:T(8,128)S(1)} %get-tuple-element.6), kind=kLoop, calls=%fused_computation | loop fusion | flops 221184 | bytes 1769476 | tf_op jit(solution)/shard_map/mul | solution.py:566

commit v7 on v6

--- a/solution.py
+++ b/solution.py
@@ -465,8 +465,6 @@
     y_puts[1](2, 1, B)
     y_puts[1](2, -1, A)
     grad_images(0, 5)
-    loss_get(0)
-    loss_send(1)
     y_puts[1](2, 1, A)
     y_puts[1](2, -1, B)
     z_put(2, 1, A)
@@ -477,14 +475,14 @@
     y_puts[0](2, 1, B)
     z_put(3, 1, B)
     z_put(3, -1, A)
-    loss_get(1)
-    loss_send(2)
+    loss_get(0)
+    loss_send(1)
     z_put(3, 1, A)
     z_put(3, -1, B)
     y_finish(1, A)
     y_finish(1, B)
-    loss_get(2)
-    loss_send(3)
+    loss_get(1)
+    loss_send(2)
     z_put(4, 1, B)
     z_put(4, -1, A)
     twin_get(1, A)
@@ -492,6 +490,8 @@
     twin_get(1, B)
     x_put(OPPOSITE, B)
     x_put(FAR, B)
+    loss_get(2)
+    loss_send(3)
     y_finish(0, A)
     z_put(4, 1, A)
     z_put(4, -1, B)

time: 68.3 us -> 68.3 us (level)
  no operation moved by 1% of the time
where the time goes in v7:
time: 68.3 us; the launch traced here: 67.5 us
  Pallas kernels  62.8 us (92%)
  between operations  3.74 us (5%)
  other arithmetic  0.97 us (1%)
    pallas_call x1, Pallas kernels, shards(): pl.pallas_call(functools.partial(kernel, float(total_pairs)), out_shape=(...  62.8 us

profile of v7, /device:TPU:1, one launch (start us, length us, event | category | flops | bytes accessed | tf_op | source)
XLA Modules:
  0.0 67.5 jit_solution(883671427132912956)
XLA Ops:
  2.0 62.8 %shard_map.85 = (f32[1,96,1152]{2,1,0:T(8,128)S(1)}, f32[1,96,1152]{2,1,0:T(8,128)S(1)}, f32[1]{0:T(128)}) custom-call(s32[4]{0:T(128)} %partner_in.1, f32[1]{0:T(128)S(6)} %copy.10.temp_in, f32[1]{0:T(128)S(6)} %copy.11.bias_in, bf16[1,96,1152]{2,1,0:T(8,128)(2,1)} %img_in.1, bf16[1,96,1152]{2,1,0:T(8,128)(2,1)} %txt_in.1, s32[1,96]{1,0:T(1,128)} %lab_in.1), custom_call_target="tpu_custom_call" | custom-call | tf_op jit(solution)/shard_map/pallas_call | solution.py:527
  64.7 1.0 %broadcast_multiply_fusion = (f32[1,96,1152]{2,1,0:T(8,128)}, f32[1,96,1152]{2,1,0:T(8,128)}) fusion(f32[1,96,1152]{2,1,0:T(8,128)S(1)} %get-tuple-element.7, f32[]{:T(128)} %bitcast, f32[1,96,1152]{2,1,0:T(8,128)S(1)} %get-tuple-element.6), kind=kLoop, calls=%fused_computation | loop fusion | flops 221184 | bytes 1769476 | tf_op jit(solution)/shard_map/mul | solution.py:566
